TPU v7x, 256 devices: a whole 4x4x8 slice. The times are simulated.
256 devices in a mesh: dp: 128 (over z, y_lo, x, core), group: 2 (over y_hi).
Axes of the slice: x: 4, y: 4 (y_hi: 2, y_lo: 2; y = y_hi * 2 + y_lo), z: 8, core: 2. Of those that a mesh axis runs over, the one named last changes fastest.
Arguments:
- atom_feats: bfloat16 [2048, 32, 512], P(('dp', 'group')), may hold values from -6 to 6
- coords: float32 [2048, 3, 32], P(('dp', 'group')), may hold values from -6 to 6
- atom_counts: int32 [2048], P(('dp', 'group')), may hold values from 8 to 32
- positives: int32 [2048], P(('dp', 'group')), may hold values from 0 to 2047, each once
- z2: bfloat16 [2048, 128], P(('dp', 'group')), may hold values from -6 to 6
- w_qkv: bfloat16 [512, 1536], replicated, may hold values from -0.25 to 0.25
- w_out: bfloat16 [512, 512], replicated, may hold values from -0.25 to 0.25
- proj: bfloat16 [512, 128], replicated, may hold values from -0.25 to 0.25
- bias_weight: float32 [128, 64], replicated, may hold values from -2 to 36
- ln_gain: float32 [512], replicated, may hold values from 0.5 to 1.5
Outputs:
- loss: float32 [], replicated
- grad_z2: float32 [2048, 128], P(('dp', 'group'))
- grad_w_qkv: float32 [512, 1536], replicated
- grad_w_out: float32 [512, 512], replicated
- grad_proj: float32 [512, 128], replicated
- grad_bias_weight: float32 [128, 64], replicated
- grad_ln_gain: float32 [512], replicated
Inputs may be any that keep to these rules, and one draw needn't show every extreme that they name: positives is a permutation of the 2048 molecules.
All inputs are finite; a program needn't handle non-finite values.
Results may differ from a plain program's by a relative error of at most 0.014.
Values may be sent and summed in bfloat16 or wider, within the bound.
A program may use at most 128 MiB of HBM per device.

v0:
```python
import math

import jax
import jax.numpy as jnp
from jax import lax
from jax.sharding import PartitionSpec as P


def pair_distance(coords):
    offsets = coords[:, :, :, None] - coords[:, :, None, :]
    return jnp.sqrt(jnp.sum(offsets * offsets, axis=1) + 0.25)


def kernel_values(distance, kernels):
    centers = jnp.arange(kernels).astype(jnp.float32) * (12.0 / kernels)
    return jnp.exp(-(((distance[..., None] - centers) / 0.5) ** 2))


def group_split(values, width):
    return values.reshape((values.shape[0] // width, width) + values.shape[1:])


def bias_forward(distance, bias_weight):
    mol_count = distance.shape[0]
    width = math.gcd(mol_count, 8)

    def one_group(group_distance):
        basis = kernel_values(group_distance, bias_weight.shape[0])
        return jnp.einsum("mijk,kh->mhij", basis, bias_weight, precision=lax.Precision.HIGHEST)

    biased = lax.map(one_group, group_split(distance, width))
    return biased.reshape((mol_count,) + biased.shape[2:])


def bias_backward(distance, bias_slope, kernels):
    width = math.gcd(distance.shape[0], 8)

    def add_group(running, pieces):
        basis = kernel_values(pieces[0], kernels)
        return (
            running
            + jnp.einsum("mijk,mhij->kh", basis, pieces[1], precision=lax.Precision.HIGHEST),
            None,
        )

    start_sum = jnp.zeros((kernels, bias_slope.shape[1]), jnp.float32)
    summed, unused = lax.scan(
        add_group, start_sum, (group_split(distance, width), group_split(bias_slope, width))
    )
    return summed


def encode_core(params_in, pair_bias, feats, counts):
    w_qkv, w_out, proj, ln_gain = params_in
    mol_count, atom_count, model_width = feats.shape
    head_count = pair_bias.shape[1]
    head_dim = model_width // head_count
    inputs = feats.astype(jnp.float32)
    center = jnp.mean(inputs, axis=-1, keepdims=True)
    spread = jnp.mean((inputs - center) ** 2, axis=-1, keepdims=True)
    normed = ((inputs - center) * lax.rsqrt(spread + 1e-05) * ln_gain).astype(jnp.bfloat16)
    projected = jnp.dot(
        normed.reshape(mol_count * atom_count, model_width),
        w_qkv,
        preferred_element_type=jnp.float32,
    ).astype(jnp.bfloat16)
    projected = projected.reshape(mol_count, atom_count, 3, head_count, head_dim)
    query_heads = projected[:, :, 0]
    key_heads = projected[:, :, 1]
    value_heads = projected[:, :, 2]
    scores = (
        jnp.einsum("mihd,mjhd->mhij", query_heads, key_heads, preferred_element_type=jnp.float32)
        * head_dim ** (-0.5)
        + pair_bias
    )
    is_valid = jnp.arange(atom_count)[None, :] < counts[:, None]
    scores = jnp.where(is_valid[:, None, None, :], scores, -1e30)
    highest = jnp.max(scores, axis=-1, keepdims=True)
    expo = jnp.exp(scores - highest)
    attn_weights = (expo / jnp.sum(expo, axis=-1, keepdims=True)).astype(jnp.bfloat16)
    context = jnp.einsum(
        "mhij,mjhd->mihd", attn_weights, value_heads, preferred_element_type=jnp.float32
    ).astype(jnp.bfloat16)
    hidden = inputs + jnp.dot(
        context.reshape(mol_count * atom_count, model_width),
        w_out,
        preferred_element_type=jnp.float32,
    ).reshape(mol_count, atom_count, model_width)
    pooled = jnp.sum(jnp.where(is_valid[..., None], hidden, 0.0), axis=1)
    return jnp.dot(pooled.astype(jnp.bfloat16), proj, preferred_element_type=jnp.float32)


def unit_rows(values):
    inverse = lax.rsqrt(jnp.mean(values * values, axis=1, keepdims=True) + 1e-06) * values.shape[
        1
    ] ** (-0.5)
    return (values * inverse, inverse)


def unit_backward(values, inverse, grad):
    along = jnp.sum(values * grad, axis=1, keepdims=True)
    return inverse * (grad - values * along * (inverse * inverse))


def on_device(
    atom_feats, coords, atom_counts, positives, z2, w_qkv, w_out, proj, bias_weight, ln_gain
):
    distance = pair_distance(coords)
    pair_bias = bias_forward(distance, bias_weight)

    def local_encode(params_in, bias_in):
        return encode_core(params_in, bias_in, atom_feats, atom_counts)

    z3, pullback = jax.vjp(local_encode, (w_qkv, w_out, proj, ln_gain), pair_bias)
    unit, inverse = unit_rows(z3)
    z3_half = unit.astype(jnp.bfloat16)
    z2_all = lax.all_gather(z2, ("dp", "group"), axis=0, tiled=True)
    batch_rows = z2_all.shape[0]
    logits = jnp.dot(z3_half, z2_all.T, preferred_element_type=jnp.float32)
    expo = jnp.exp(logits)
    row_lse = jnp.log(jnp.sum(expo, axis=1))
    columns = jnp.arange(batch_rows)
    is_positive = positives[:, None] == columns[None, :]
    positive_score = jnp.sum(jnp.where(is_positive, logits, 0.0), axis=1)
    local_sum = jnp.sum(0.5 * row_lse - positive_score)
    col_total = lax.psum(jnp.sum(expo, axis=0), ("dp", "group"))
    col_lse = jnp.log(col_total)
    column_part = 0.5 * jnp.sum(col_lse)
    slope = (
        0.5 * jnp.exp(logits - row_lse[:, None])
        + 0.5 * jnp.exp(logits - col_lse[None, :])
        - is_positive.astype(jnp.float32)
    ).astype(jnp.bfloat16)
    grad_z2 = lax.psum_scatter(
        lax.dot_general(
            slope, z3_half, (((0,), (0,)), ((), ())), preferred_element_type=jnp.float32
        ),
        ("dp", "group"),
        scatter_dimension=0,
        tiled=True,
    )
    grad_unit = jnp.dot(slope, z2_all, preferred_element_type=jnp.float32)
    grad_z3 = unit_backward(z3, inverse, grad_unit)
    pieces, bias_slope = pullback(grad_z3)
    grad_bias = bias_backward(distance, bias_slope, bias_weight.shape[0])
    totals = lax.psum(
        (
            local_sum,
            pieces[0].astype(jnp.float32),
            pieces[1].astype(jnp.float32),
            pieces[2].astype(jnp.float32),
            grad_bias,
            pieces[3],
        ),
        ("dp", "group"),
    )
    loss = (totals[0] + column_part) / batch_rows
    return (loss, grad_z2, totals[1], totals[2], totals[3], totals[4], totals[5])


def solution(mesh):
    return jax.shard_map(
        on_device,
        mesh=mesh,
        in_specs=(
            P(("dp", "group"), None, None),
            P(("dp", "group"), None, None),
            P(("dp", "group")),
            P(("dp", "group")),
            P(("dp", "group"), None),
            P(),
            P(),
            P(),
            P(),
            P(),
        ),
        out_specs=(P(), P(("dp", "group"), None), P(), P(), P(), P(), P()),
        check_vma=False,
    )
```

profile of v0, /device:TPU:1, one launch (start us, length us, event | category | flops | bytes accessed | tf_op | source)
XLA Modules:
  0.0 1102.2 jit_solution(12725409746250518894)
XLA Ops:
  7.2 0.0 copy-start
  7.2 0.0 all-reduce.8.cloned.1.call-start
  7.2 1.2 convert_reduce_fusion.1
  8.4 1.2 fusion.44
  9.6 1.1 fusion.42
  10.7 0.7 copy-done.13
  11.4 0.6 convolution_convert_fusion.2
  12.0 0.3 copy.69
  12.3 2.8 reshape.179
  15.1 3.9 fusion.58
  19.1 0.1 iota_compare_fusion.1
  19.2 0.2 multiply_reduce_fusion
  19.4 0.1 copy.75
  19.5 0.6 copy-done.21
  20.1 5.4 fusion.10
  25.5 9.2 copy.77
  34.7 7.3 fusion.60
  41.9 2.7 fusion.9
  44.6 0.5 copy-done.1
  45.2 2.3 divide_convert_fusion
  47.5 1.2 convolution_convert_fusion.4
  48.7 0.4 copy-done.15
  49.1 0.5 fusion.31
  49.6 0.2 multiply_reduce_fusion.2
  49.9 629.5 %all_gather.3 = bf16[2048,128]{1,0:T(8,128)(2,1)S(1)} all-gather(bf16[8,128]{1,0:T(8,128)(2,1)S(1)} %copy-done.25), channel_id=1, replica_groups=mesh['dp'=128,'group'=2] {'dp','group'}, dimensions={0}, use_global_device_ids=true | all-gather | bytes 526336 | tf_op jit(solution)/shard_map/all_gather | solution.py:117
  679.4 0.8 copy-done.12
  680.2 0.4 exponential_reduce_fusion
  680.6 74.2 %psum.50 = f32[2048]{0:T(1024)S(1)} all-reduce(f32[2048]{0:T(1024)S(1)} %get-tuple-element.27), channel_id=1, replica_groups=mesh['dp'=128,'group'=2] {'dp','group'}, use_global_device_ids=true, to_apply=%region_12.13 | all-reduce | flops 2048 | bytes 16384 | tf_op jit(solution)/shard_map/psum | solution.py:126
  754.8 0.6 log_reduce_fusion
  755.4 0.6 fusion.59
  756.0 1.4 multiply_reduce_fusion.1
  757.4 1.0 fusion.32
  758.4 1.1 fusion.34
  759.5 0.1 lt.30
  759.6 0.8 multiply_divide_fusion
  760.3 0.8 broadcast_select_fusion
  761.1 0.1 bitcast_select_fusion
  761.2 2.1 fusion.61
  763.3 1.8 copy.80
  765.1 2.4 reshape.180
  767.5 5.9 fusion.21
  773.5 5.8 fusion.3
  779.4 8.8 convert_reduce_fusion
  788.2 6.1 add_select_fusion
  794.3 3.7 fusion.25
  798.1 2.2 fusion.22
  800.2 1.4 fusion.53
  801.7 1.2 copy.87
  802.9 0.7 reshape.182
  803.6 2.7 pad_add_fusion
  806.3 5.3 copy.86
  811.6 4.3 reshape.181
  815.9 2.3 fusion.14
  818.2 1.3 fusion.28
  819.5 0.0 all-reduce.8.cloned.1.call-update
  819.5 0.6 fusion.43
  820.1 9.0 copy.88
  829.1 10.4 fusion.33
  839.5 75.8 %all-reduce.4 = (f32[]{:T(128)}, f32[128,64]{0,1:T(8,128)}, f32[512]{0:T(512)}) all-reduce(f32[]{:T(128)} %get-tuple-element.52, f32[128,64]{0,1:T(8,128)S(1)} %fusion.33, f32[512]{0:T(512)S(1)} %fusion.43), channel_id=1, replica_groups=mesh['dp'=128,'group'=2] {'dp','group'}, use_global_device_ids=true, to_apply=%region_10.11 | all-reduce | flops 8705 | bytes 69640 | tf_op jit(solution)/shard_map/psum | solution.py:146
  916.6 170.6 %all-reduce.8.cloned.1.call-done = (f32[2048,128]{1,0:T(8,128)}, f32[512,1536]{1,0:T(8,128)}, f32[512,512]{1,0:T(8,128)}, f32[512,128]{1,0:T(8,128)}) async-done(((f32[2048,128]{1,0:T(8,128)}, f32[512,1536]{1,0:T(8,128)}, f32[512,512]{1,0:T(8,128)}, f32[512,128]{1,0:T(8,128)}), (f32[2048,128]{1,0:T(8,128)}, f32[512,1536]{1,0:T(8,128)}, f32[512,512]{1,0:T(8,128)}, ...) | async-done | bytes 5505040
  1087.2 1.4 constant_dynamic-slice_fusion
  1088.6 3.8 copy.126
  1092.4 1.0 copy.127
  1093.4 0.7 copy.128
  (63 shorter events, 0.3 us)
Async XLA Ops:
  7.2 4.3 copy-start
  7.2 1080.0 %all-reduce.8.cloned.1.call-start = ((), (), s32[]{:S(2)}) async-start(), calls=%async_computation | async-start | bytes 11010048
  10.7 0.7 copy-start.13
  12.3 6.8 copy-start.27
  12.3 6.9 copy-start.23
  15.1 5.0 copy-start.26
  19.5 0.6 copy-start.21
  41.9 3.2 copy-start.1
  45.2 2.3 copy-start.9
  47.4 631.9 %copy-start.3 = (bf16[8,64,32,32]{2,3,1,0:T(8,128)(2,1)}, bf16[8,64,32,32]{2,3,1,0:T(8,128)(2,1)S(1)}, u32[]{:S(2)}) copy-start(bf16[8,64,32,32]{2,3,1,0:T(8,128)(2,1)S(1)} %divide_convert_fusion) | copy-start | bytes 3145732
  47.4 1.3 copy-start.11
  47.5 1.7 copy-start.15
  47.5 2.1 copy-start.20
  47.5 2.4 copy-start.25
  47.5 632.7 %copy-start.24 = (s32[8]{0:T(128)S(1)}, s32[8]{0:T(128)}, u32[]{:S(2)}) copy-start(s32[8]{0:T(128)} %param.13) | copy-start | bytes 100
  49.1 630.2 %copy-start.6 = (bf16[8,64,8,32]{3,2,1,0:T(8,128)(2,1)}, bf16[8,64,8,32]{3,2,1,0:T(8,128)(2,1)S(1)}, u32[]{:S(2)}) copy-start(bf16[8,64,8,32]{3,2,1,0:T(8,128)(2,1)S(1)} %convolution_convert_fusion.4) | copy-start | bytes 786436
  679.4 0.8 copy-start.12
  767.5 5.9 copy-start.8
  767.5 5.9 copy-start.10
  767.5 5.9 copy-start.16
  767.5 11.8 %slice-start = ((s8[8388608]{0:T(1024)(128)(4,1)}), s8[4194304]{0:T(1024)(128)(4,1)S(1)}, s32[]{:S(2)}) async-start(s8[8388608]{0:T(1024)(128)(4,1)} %bitcast.90), calls=%async_computation.1 | async-start | bytes 8388608
  773.5 5.9 slice-start.1
  779.3 8.8 copy-start.4
  788.2 6.1 copy-start.5
  794.3 3.7 copy-start.2
  798.1 3.6 copy-start.7
  806.3 9.6 copy-start.14
  811.6 6.6 copy-start.18
  820.1 9.0 copy-start.22
  1087.2 5.2 copy-start.17
  1088.6 4.8 copy-start.19
Sparse Core Ops, SparseCore 0:
  819.6 267.5 all-reduce.7
where the time goes:
time: 1110 us; the launch traced here: 1100 us
  blocking collectives  779 us (70%)
  waiting for transfers between devices  171 us (15%)
  matrix products  54.7 us (5%)
  local copies, waits for them, and re-layouts  51.1 us (5%)
  other arithmetic  29.1 us (3%)
  between operations  17.1 us (2%)
    all_gather x1, blocking collectives, on_device(): z2_all = lax.all_gather(z2, ('dp', 'group'), axis=0, tiled=True)  629 us
    unnamed x2, waiting for transfers between devices  171 us
    psum x1, blocking collectives, on_device(): lax.psum((local_sum, pieces[0].astype(jnp.float32), pieces[1].astype(jnp....  75.8 us
    psum x1, blocking collectives, on_device(): col_total = lax.psum(jnp.sum(expo, axis=0), ('dp', 'group'))  74.2 us
  transfers between devices with their start and end apart: 1, of which 1 were waited for; matrix products, arithmetic and copies ran while one was open for 2% of the time, Pallas kernels for 0%

commit v1 on v0

v1 whole, which is shorter than its diff:
```python
import functools

import jax
import jax.numpy as jnp
from jax import lax
from jax.experimental import pallas as pl
from jax.experimental.pallas import tpu as pltpu
from jax.sharding import PartitionSpec as P

MESH = pl.DeviceIdType.MESH
F32 = jnp.float32
BF = jnp.bfloat16

MOLS = 8
PAIRS = 4
ATOMS = 32
WIDTH = 512
HEADS = 64
HEAD_DIM = 8
KERNELS = 128
LANES = 128
WIDE = HEAD_DIM * LANES
BATCH = 2048
SIDE = 16
DEPTH = 8
PAYLOAD = 2048

Z2, POS, Z3, ROWS, COLS, UNIT, GZ2, CORE, PLANE, RING, RING_OUT, PLANE_OUT, CORE_OUT = range(13)


def mm(a, b):
    return lax.dot_general(a, b, (((1,), (0,)), ((), ())), preferred_element_type=F32)


def mm_t(a, b):
    return lax.dot_general(a, b, (((1,), (1,)), ((), ())), preferred_element_type=F32)


def tmm(a, b):
    return lax.dot_general(a, b, (((0,), (0,)), ((), ())), preferred_element_type=F32)


def halves(values):
    high = values.astype(BF)
    return high, (values - high.astype(F32)).astype(BF)


def stacked(values):
    high = values.astype(BF).astype(F32)
    return jnp.concatenate([high, values - high], axis=0).astype(BF)


def two_part(values, weights, product):
    rows = values.shape[0]
    both = product(stacked(values), weights)
    return both[:rows] + both[rows:]


def lane_is_odd(shape):
    return (lax.broadcasted_iota(jnp.int32, shape, len(shape) - 1) & 64) != 0


def device_of(place):
    return (place // 2, place % 2)


def remote(src, dst, sems, kind, slot, place):
    return pltpu.make_async_remote_copy(
        src_ref=src,
        dst_ref=dst,
        send_sem=sems[0].at[kind, slot],
        recv_sem=sems[1].at[kind, slot],
        device_id=device_of(place),
        device_id_type=MESH,
    )


def forward(feats, coords, counts, wqkv, wout, proj, bias_weight, gain, s):
    x = feats[...].astype(F32)
    mean = jnp.mean(x, axis=-1, keepdims=True)
    centred = x - mean
    var = jnp.mean(centred * centred, axis=-1, keepdims=True)
    xhat = centred * lax.rsqrt(var + 1e-05)
    s.xhat[...] = xhat
    normed = (xhat * gain[...]).astype(BF)
    s.normed[...] = normed
    for m in range(MOLS):
        valid = lax.broadcasted_iota(jnp.int32, (ATOMS, WIDTH), 0) < counts[m]
        s.xsum[m : m + 1, :] = jnp.sum(
            jnp.where(valid, x[m * ATOMS : (m + 1) * ATOMS], 0.0), axis=0, keepdims=True
        )

    row = lax.broadcasted_iota(jnp.int32, (WIDTH, WIDE), 0)
    col = lax.broadcasted_iota(jnp.int32, (WIDTH, WIDE), 1)
    placed = ((row >> 3) == (col & 63)) & ((row & 7) == (col >> 7))
    s.perm[...] = jnp.where(placed, 1.0, 0.0).astype(BF)

    odd = lane_is_odd((ATOMS, WIDE))
    for part, (target, scale) in enumerate(((s.q, HEAD_DIM ** (-0.5)), (s.k, 1.0), (s.v, 1.0))):
        projected = mm(normed, wqkv[:, part * WIDTH : (part + 1) * WIDTH]).astype(BF)
        spread = mm(projected, s.perm[...])
        for p in range(PAIRS):
            low = spread[(2 * p) * ATOMS : (2 * p + 1) * ATOMS]
            high = spread[(2 * p + 1) * ATOMS : (2 * p + 2) * ATOMS]
            merged = jnp.where(odd, high, low)
            target[p] = merged * scale if scale != 1.0 else merged

    atom = lax.broadcasted_iota(jnp.int32, (ATOMS, ATOMS * ATOMS), 0)
    pair = lax.broadcasted_iota(jnp.int32, (ATOMS, ATOMS * ATOMS), 1)
    select = (
        jnp.where(atom == (pair & 31), 1.0, 0.0) - jnp.where(atom == (pair >> 5), 1.0, 0.0)
    ).astype(BF)
    squared = jnp.zeros((MOLS, ATOMS * ATOMS), F32)
    for c in range(3):
        values = coords[c]
        first = values.astype(BF).astype(F32)
        second = (values - first).astype(BF).astype(F32)
        third = values - first - second
        three = mm(jnp.concatenate([first, second, third], axis=0).astype(BF), select)
        offset = three[:MOLS] + three[MOLS : 2 * MOLS] + three[2 * MOLS :]
        squared = squared + offset * offset
    distance = jnp.sqrt(squared + 0.25)
    for m in range(MOLS):
        s.distance[m] = distance[m : m + 1]

    wide = jnp.concatenate([bias_weight[...], bias_weight[...]], axis=1)
    turned = wide.T
    upper = lax.broadcasted_iota(jnp.int32, (LANES, KERNELS), 0) < HEADS
    blocks = jnp.concatenate([jnp.where(upper, turned, 0.0), jnp.where(upper, 0.0, turned)], axis=1)
    s.bias_lhs[...] = stacked(blocks)

    centers = lax.broadcasted_iota(jnp.int32, (KERNELS, 2 * LANES), 0).astype(F32) * (12.0 / KERNELS)

    def one_pair(p, carry):
        count = jnp.where(lane_is_odd((1, LANES)), counts[2 * p + 1], counts[2 * p])
        for block in range(4):
            at = pl.ds(block * 256, 256)
            basis = []
            for parity in range(2):
                away = (s.distance[2 * p + parity, :, at] - centers) * 2.0
                basis.append(jnp.exp(-(away * away)))
            high, low = halves(jnp.concatenate(basis, axis=0))
            s.basis[p, :, at] = high
            both = mm(s.bias_lhs[...], high)
            bias = both[:LANES] + both[LANES:] + mm(s.bias_lhs[:LANES, :], low)
            s.attn[p, at, :] = bias.T
        top = jnp.full((ATOMS, LANES), -1e30, F32)
        for j in range(ATOMS):
            at = pl.ds(j * ATOMS, ATOMS)
            score = s.attn[p, at, :]
            for d in range(HEAD_DIM):
                lanes = pl.ds(d * LANES, LANES)
                score = score + s.q[p, :, lanes] * s.k[p, j : j + 1, lanes]
            score = jnp.where(j < count, score, -1e30)
            s.attn[p, at, :] = score
            top = jnp.maximum(top, score)
        total = jnp.zeros((ATOMS, LANES), F32)
        for j in range(ATOMS):
            at = pl.ds(j * ATOMS, ATOMS)
            expo = jnp.exp(s.attn[p, at, :] - top)
            s.attn[p, at, :] = expo
            total = total + expo
        real = lax.broadcasted_iota(jnp.int32, (ATOMS, LANES), 0) < count
        share = jnp.where(real, 1.0 / total, 0.0)
        for j in range(ATOMS):
            at = pl.ds(j * ATOMS, ATOMS)
            weight = s.attn[p, at, :] * share
            s.attn[p, at, :] = weight
            s.column[p, j : j + 1, :] = jnp.sum(weight, axis=0, keepdims=True)
        odd_row = lane_is_odd((1, LANES))
        for d in range(HEAD_DIM):
            lanes = pl.ds(d * LANES, LANES)
            context = jnp.sum(s.column[p] * s.v[p, :, lanes], axis=0, keepdims=True)
            s.context[2 * p, :, lanes] = jnp.where(odd_row, 0.0, context)
            s.context[2 * p + 1, :, lanes] = jnp.where(odd_row, context, 0.0)
        return carry

    lax.fori_loop(0, PAIRS, one_pair, 0)
    context = jnp.concatenate([s.context[m] for m in range(MOLS)], axis=0)
    context = two_part(context, s.perm[...], mm_t)
    s.ctx_sum[...] = context
    pooled = (s.xsum[...] + two_part(context, wout[...], mm)).astype(BF)
    s.pooled[...] = pooled.astype(F32)
    return mm(pooled, proj[...])


def backward(grad_z3, wqkv, wout, proj, s):
    cs_high, cs_low = halves(s.ctx_sum[...])
    g_high, g_low = halves(grad_z3)
    f = lambda v: v.astype(F32)
    left = jnp.concatenate([f(cs_high), f(cs_low), f(cs_high)], axis=0).astype(BF)
    right = jnp.concatenate([f(g_high), f(g_high), f(g_low)], axis=0).astype(BF)
    s.payload[:, 1536:1664] = tmm(left, right).astype(BF)
    left = jnp.concatenate([s.pooled[...], s.pooled[...]], axis=0).astype(BF)
    right = jnp.concatenate([f(g_high), f(g_low)], axis=0).astype(BF)
    s.payload[:, 1664:1792] = tmm(left, right).astype(BF)

    grad_pooled = two_part(grad_z3, proj[...], mm_t)
    grad_ctx = two_part(grad_pooled, wout[...], mm_t)
    spread = two_part(grad_ctx, s.perm[...], mm)
    for m in range(MOLS):
        s.context[m] = spread[m : m + 1]

    scale = HEAD_DIM ** (-0.5)
    odd_row = lane_is_odd((1, LANES))

    def one_pair(p, bias_sum):
        along = jnp.zeros((ATOMS, LANES), F32)
        for d in range(HEAD_DIM):
            lanes = pl.ds(d * LANES, LANES)
            grad = jnp.where(
                odd_row, s.context[2 * p + 1, :, lanes], s.context[2 * p, :, lanes]
            )
            along = along + grad * s.v[p, :, lanes]
            s.dv[p, :, lanes] = (s.column[p] * grad).astype(BF)
        s.along[...] = along
        mean = jnp.zeros((ATOMS, LANES), F32)
        for j in range(ATOMS):
            mean = mean + s.attn[p, pl.ds(j * ATOMS, ATOMS), :] * s.along[j : j + 1, :]
        for d in range(HEAD_DIM):
            s.dq[:, pl.ds(d * LANES, LANES)] = jnp.zeros((ATOMS, LANES), F32)
        for half in range(2):
            ds_range = range(4 * half, 4 * half + 4)
            sums = [jnp.zeros((ATOMS, LANES), F32) for d in ds_range]
            for j in range(ATOMS):
                at = pl.ds(j * ATOMS, ATOMS)
                if half == 0:
                    slope = s.attn[p, at, :] * (s.along[j : j + 1, :] - mean)
                    s.attn[p, at, :] = slope
                else:
                    slope = s.attn[p, at, :]
                for n, d in enumerate(ds_range):
                    lanes = pl.ds(d * LANES, LANES)
                    sums[n] = sums[n] + slope * s.k[p, j : j + 1, lanes]
                    s.dk[j : j + 1, lanes] = jnp.sum(slope * s.q[p, :, lanes], axis=0, keepdims=True)
            for n, d in enumerate(ds_range):
                s.dq[:, pl.ds(d * LANES, LANES)] = sums[n] * scale
        s.dqs[p] = s.dq[...].astype(BF)
        s.dks[p] = s.dk[...].astype(BF)
        return bias_sum + mm(s.basis[p], s.attn[p].astype(BF))

    bias_sum = lax.fori_loop(0, PAIRS, one_pair, jnp.zeros((2 * KERNELS, LANES), F32))
    odd = lane_is_odd((KERNELS, LANES))
    folded = jnp.where(odd, bias_sum[KERNELS:], bias_sum[:KERNELS])
    folded = folded + pltpu.roll(folded, 64, 1)
    s.small[...] = jnp.zeros((WIDTH, LANES), F32)
    s.small[0:64, :] = jnp.where(lane_is_odd((64, LANES)), folded[64:], folded[:64])

    odd = lane_is_odd((ATOMS, WIDE))
    zero = jnp.zeros((ATOMS, WIDE), BF)
    for part, source in enumerate((s.dqs, s.dks, s.dv)):
        pieces = []
        for m in range(MOLS):
            value = source[m // 2]
            pieces.append(jnp.where(odd, value, zero) if m % 2 else jnp.where(odd, zero, value))
        s.dproj[:, part * WIDTH : (part + 1) * WIDTH] = mm_t(
            jnp.concatenate(pieces, axis=0), s.perm[...]
        ).astype(BF)
    for part in range(3):
        at = pl.ds(part * WIDTH, WIDTH)
        s.payload[:, at] = tmm(s.normed[...], s.dproj[:, at]).astype(BF)
    grad_normed = mm_t(s.dproj[...], wqkv[...])
    grad_gain = jnp.sum(grad_normed * s.xhat[...], axis=0, keepdims=True)
    for n in range(4):
        s.small[64 + n : 65 + n, :] = grad_gain[:, n * LANES : (n + 1) * LANES]


def fused(
    counts,
    positives,
    feats,
    coords,
    z2,
    wqkv,
    wout,
    proj,
    bias_weight,
    gain,
    summed,
    grad_z2,
    *scratch,
):
    s = Scratch(scratch)
    sems = (s.send, s.recv)
    me = lax.axis_index("dp") * 2 + lax.axis_index("group")
    row_group, col_group = me // SIDE, me % SIDE
    core = (me // 2) % 2
    sibling = me + 2 - 4 * core
    plane = ((me // 16) % 2) * 8 + ((me // 4) % 4) * 2 + me % 2
    ring = me // 32

    def along_row(n):
        return row_group * SIDE + n

    def along_col(n):
        return n * SIDE + col_group

    def in_plane(n):
        return ring * 32 + (n // 8) * 16 + ((n // 2) % 4) * 4 + core * 2 + n % 2

    def in_ring(n):
        return n * 32 + me % 32

    barrier = pltpu.get_barrier_semaphore()

    def signal(place):
        pl.semaphore_signal(barrier, inc=1, device_id=device_of(place), device_id_type=MESH)

    def greet(o, carry):
        signal(along_row((col_group + o) % SIDE))
        signal(along_col((row_group + o) % SIDE))
        signal(in_plane((plane + o) % SIDE))
        return carry

    lax.fori_loop(1, SIDE, greet, 0)

    def greet_ring(o, carry):
        signal(in_ring((ring + o) % DEPTH))
        return carry

    lax.fori_loop(1, DEPTH, greet_ring, 0)
    signal(sibling)
    pl.semaphore_wait(barrier, 3 * (SIDE - 1) + (DEPTH - 1) + 1)

    def slot(n):
        return pl.ds(n * 8, 8)

    def each(count, body):
        def step(o, carry):
            body(o)
            return carry

        lax.fori_loop(1, count, step, 0)

    s.z2[slot(row_group), :] = z2[...].astype(F32)
    targets = jnp.zeros((8, LANES), jnp.int32)
    sub = lax.broadcasted_iota(jnp.int32, (8, LANES), 0)
    for n in range(8):
        targets = jnp.where(sub == n, positives[n], targets)
    s.pos[slot(col_group), :] = targets

    def z2_copy(o):
        mine = s.z2.at[slot(row_group), :]
        return remote(mine, mine, sems, Z2, o, along_col((row_group + o) % SIDE))

    def pos_copy(o):
        mine = s.pos.at[slot(col_group), :]
        return remote(mine, mine, sems, POS, o, along_row((col_group + o) % SIDE))

    def z3_copy(o):
        mine = s.z3.at[slot(col_group), :]
        return remote(mine, mine, sems, Z3, o, along_row((col_group + o) % SIDE))

    def rows_copy(o):
        mine = s.rows.at[col_group]
        return remote(mine, mine, sems, ROWS, o, along_row((col_group + o) % SIDE))

    def cols_copy(o):
        mine = s.cols.at[row_group]
        return remote(mine, mine, sems, COLS, o, along_col((row_group + o) % SIDE))

    def unit_copy(o):
        peer = (col_group + o) % SIDE
        return remote(s.unit.at[peer], s.unit_in.at[col_group], sems, UNIT, o, along_row(peer))

    def gz2_copy(o):
        peer = (row_group + o) % SIDE
        return remote(s.gz2.at[peer], s.gz2_in.at[row_group], sems, GZ2, o, along_col(peer))

    each(SIDE, lambda o: z2_copy(o).start())
    each(SIDE, lambda o: pos_copy(o).start())

    z3 = forward(feats, coords, counts, wqkv, wout, proj, bias_weight, gain, s)
    inverse = lax.rsqrt(jnp.mean(z3 * z3, axis=1, keepdims=True) + 1e-06) * LANES ** (-0.5)
    s.z3[slot(col_group), :] = (z3 * inverse).astype(BF).astype(F32)
    each(SIDE, lambda o: z3_copy(o).start())
    each(SIDE, lambda o: z2_copy(o).wait())
    each(SIDE, lambda o: pos_copy(o).wait())
    each(SIDE, lambda o: z3_copy(o).wait())

    z3_all = s.z3[...].astype(BF)
    z2_all = s.z2[...].astype(BF)
    logits = mm_t(z3_all, z2_all)
    expo = jnp.exp(logits)
    expo_t = jnp.exp(mm_t(z2_all, z3_all))
    s.rows[col_group] = jnp.broadcast_to(jnp.sum(expo_t, axis=0, keepdims=True), (8, LANES))
    s.cols[row_group] = jnp.broadcast_to(jnp.sum(expo, axis=0, keepdims=True), (8, LANES))
    each(SIDE, lambda o: rows_copy(o).start())
    each(SIDE, lambda o: cols_copy(o).start())
    lane = lax.broadcasted_iota(jnp.int32, (LANES, LANES), 1)
    column_id = (lane >> 3) * LANES + col_group * 8 + (lane & 7)
    hit = s.pos[...] == column_id
    score = jnp.sum(jnp.where(hit, logits, 0.0), axis=0, keepdims=True)
    each(SIDE, lambda o: rows_copy(o).wait())
    each(SIDE, lambda o: cols_copy(o).wait())
    row_sum = s.rows[0]
    col_sum = s.cols[0]
    for n in range(1, SIDE):
        row_sum = row_sum + s.rows[n]
        col_sum = col_sum + s.cols[n]
    row_half = jnp.broadcast_to(0.5 / row_sum[0:1], (LANES, LANES)).T
    slope = expo * (row_half + 0.5 / col_sum[0:1]) - jnp.where(hit, 1.0, 0.0)
    unit = mm(slope.astype(BF), z2_all)
    for n in range(SIDE):
        s.unit[n] = unit[n * 8 : (n + 1) * 8]
    s.unit_in[col_group] = s.unit[col_group]
    each(SIDE, lambda o: unit_copy(o).start())
    grad_cols = tmm(slope.astype(BF), z3_all)
    for n in range(SIDE):
        s.gz2[n] = grad_cols[n * 8 : (n + 1) * 8]
    s.gz2_in[row_group] = s.gz2[row_group]
    each(SIDE, lambda o: gz2_copy(o).start())
    one_lane = lax.broadcasted_iota(jnp.int32, (1, LANES), 1)
    row_term = jnp.where((one_lane >> 3) == col_group, 0.5 * jnp.log(row_sum[0:1]), 0.0)
    col_term = jnp.where((one_lane >> 3) == row_group, 0.5 * jnp.log(col_sum[0:1]), 0.0)
    loss_terms = row_term + col_term - score

    each(SIDE, lambda o: unit_copy(o).wait())
    grad_unit = s.unit_in[0]
    for n in range(1, SIDE):
        grad_unit = grad_unit + s.unit_in[n]
    dot = jnp.sum(z3 * grad_unit, axis=1, keepdims=True)
    grad_z3 = inverse * (grad_unit - z3 * dot * (inverse * inverse))

    backward(grad_z3, wqkv, wout, proj, s)
    s.small[68:69, :] = loss_terms
    s.payload[:, 1792:1920] = s.small[...].astype(BF)
    s.payload[:, 1920:2048] = jnp.zeros((WIDTH, LANES), BF)

    def piece(half, n):
        return pl.ds(half * 256 + n * 16, 16)

    def core_copy(o):
        n = (plane + o) % SIDE
        return remote(
            s.payload.at[piece(1 - core, n), :], s.core_in.at[n], sems, CORE, o, sibling
        )

    def plane_copy(o):
        n = (plane + o) % SIDE
        return remote(s.plane_out.at[n], s.plane_in.at[plane], sems, PLANE, o, in_plane(n))

    def ring_copy(o):
        n = (ring + o) % DEPTH
        return remote(
            s.ring_out.at[:, pl.ds(pl.multiple_of(n * 256, 256), 256)],
            s.ring_in.at[ring],
            sems,
            RING,
            o,
            in_ring(n),
        )

    def ring_share(o):
        mine = summed.at[piece(core, plane), pl.ds(pl.multiple_of(ring * 256, 256), 256)]
        return remote(mine, mine, sems, RING_OUT, o, in_ring((ring + o) % DEPTH))

    def plane_share(o):
        mine = summed.at[piece(core, plane), :]
        return remote(mine, mine, sems, PLANE_OUT, o, in_plane((plane + o) % SIDE))

    def core_share(o):
        mine = summed.at[piece(core, (plane - o + SIDE) % SIDE), :]
        return remote(mine, mine, sems, CORE_OUT, o, sibling)

    each(SIDE + 1, lambda o: core_copy(o).start())

    def core_sum(o):
        core_copy(o).wait_recv()
        n = (plane + o) % SIDE
        return (
            s.payload[piece(core, n), :].astype(F32) + s.core_in[n].astype(F32)
        ).astype(BF)

    def pass_on(o):
        s.plane_out[(plane + o) % SIDE] = core_sum(o)
        plane_copy(o).start()

    each(SIDE, pass_on)
    s.plane_in[plane] = core_sum(SIDE)
    each(SIDE, lambda o: plane_copy(o).wait())
    total = s.plane_in[0].astype(F32)
    for n in range(1, SIDE):
        total = total + s.plane_in[n].astype(F32)
    s.ring_out[...] = total.astype(BF)
    each(DEPTH, lambda o: ring_copy(o).start())
    s.ring_in[ring] = s.ring_out[:, pl.ds(pl.multiple_of(ring * 256, 256), 256)]
    each(DEPTH, lambda o: ring_copy(o).wait())
    total = s.ring_in[0].astype(F32)
    for n in range(1, DEPTH):
        total = total + s.ring_in[n].astype(F32)
    summed[piece(core, plane), pl.ds(pl.multiple_of(ring * 256, 256), 256)] = total.astype(BF)
    each(DEPTH, lambda o: ring_share(o).start())
    each(DEPTH, lambda o: ring_share(o).wait())
    each(SIDE, lambda o: plane_share(o).start())
    core_share(0).start()

    def forward_piece(o):
        plane_share(o).wait_recv()
        core_share(o).start()

    each(SIDE, forward_piece)
    each(SIDE, lambda o: gz2_copy(o).wait())
    total = s.gz2_in[0]
    for n in range(1, SIDE):
        total = total + s.gz2_in[n]
    grad_z2[...] = total
    each(SIDE + 1, lambda o: core_copy(o).wait_send())
    each(SIDE, lambda o: plane_share(o).wait_send())
    core_share(0).wait()
    each(SIDE, lambda o: core_share(o).wait())


SHAPES = {
    "xhat": ((256, WIDTH), F32),
    "normed": ((256, WIDTH), BF),
    "xsum": ((MOLS, WIDTH), F32),
    "perm": ((WIDTH, WIDE), BF),
    "q": ((PAIRS, ATOMS, WIDE), F32),
    "k": ((PAIRS, ATOMS, WIDE), F32),
    "v": ((PAIRS, ATOMS, WIDE), F32),
    "distance": ((MOLS, 1, ATOMS * ATOMS), F32),
    "bias_lhs": ((2 * LANES, 2 * KERNELS), BF),
    "basis": ((PAIRS, 2 * KERNELS, ATOMS * ATOMS), BF),
    "attn": ((PAIRS, ATOMS * ATOMS, LANES), F32),
    "column": ((PAIRS, ATOMS, LANES), F32),
    "context": ((MOLS, 1, WIDE), F32),
    "ctx_sum": ((MOLS, WIDTH), F32),
    "pooled": ((MOLS, WIDTH), F32),
    "along": ((ATOMS, LANES), F32),
    "dq": ((ATOMS, WIDE), F32),
    "dk": ((ATOMS, WIDE), F32),
    "dqs": ((PAIRS, ATOMS, WIDE), BF),
    "dks": ((PAIRS, ATOMS, WIDE), BF),
    "dv": ((PAIRS, ATOMS, WIDE), BF),
    "dproj": ((256, 3 * WIDTH), BF),
    "small": ((WIDTH, LANES), F32),
    "payload": ((WIDTH, PAYLOAD), BF),
    "z2": ((LANES, LANES), F32),
    "pos": ((LANES, LANES), jnp.int32),
    "z3": ((LANES, LANES), F32),
    "rows": ((SIDE, 8, LANES), F32),
    "cols": ((SIDE, 8, LANES), F32),
    "unit": ((SIDE, 8, LANES), F32),
    "unit_in": ((SIDE, 8, LANES), F32),
    "gz2": ((SIDE, 8, LANES), F32),
    "gz2_in": ((SIDE, 8, LANES), F32),
    "core_in": ((SIDE, 16, PAYLOAD), BF),
    "plane_out": ((SIDE, 16, PAYLOAD), BF),
    "plane_in": ((SIDE, 16, PAYLOAD), BF),
    "ring_out": ((16, PAYLOAD), BF),
    "ring_in": ((DEPTH, 16, 256), BF),
}


class Scratch:
    def __init__(self, refs):
        for name, ref in zip(list(SHAPES) + ["send", "recv"], refs):
            setattr(self, name, ref)


def unpack(summed, proj, g_qkv, g_out, g_proj, small):
    g_qkv[...] = summed[:, 0:1536].astype(F32)
    g_out[...] = mm_t(summed[:, 1536:1664], proj[...])
    g_proj[...] = summed[:, 1664:1792].astype(F32)
    small[...] = summed[0:80, 1792:1920].astype(F32)


def on_device(
    atom_feats, coords, atom_counts, positives, z2, w_qkv, w_out, proj, bias_weight, ln_gain
):
    vmem = pl.BlockSpec(memory_space=pltpu.VMEM)
    smem = pl.BlockSpec(memory_space=pltpu.SMEM)
    summed, grad_z2 = pl.pallas_call(
        fused,
        out_shape=(
            jax.ShapeDtypeStruct((WIDTH, PAYLOAD), BF),
            jax.ShapeDtypeStruct((8, LANES), F32),
        ),
        in_specs=[smem, smem] + [vmem] * 8,
        out_specs=(vmem, vmem),
        scratch_shapes=[pltpu.VMEM(*shape) for shape in SHAPES.values()]
        + [pltpu.SemaphoreType.DMA((13, SIDE + 1))] * 2,
        compiler_params=pltpu.CompilerParams(
            collective_id=0, has_side_effects=True, vmem_limit_bytes=56 * 1024 * 1024
        ),
        name="pretrain_step",
    )(
        atom_counts,
        positives,
        atom_feats.reshape(256, WIDTH),
        coords.transpose(1, 0, 2),
        z2,
        w_qkv,
        w_out,
        proj,
        bias_weight,
        ln_gain.reshape(1, WIDTH),
    )
    g_qkv, g_out, g_proj, small = pl.pallas_call(
        unpack,
        out_shape=(
            jax.ShapeDtypeStruct((WIDTH, 3 * WIDTH), F32),
            jax.ShapeDtypeStruct((WIDTH, WIDTH), F32),
            jax.ShapeDtypeStruct((WIDTH, LANES), F32),
            jax.ShapeDtypeStruct((80, LANES), F32),
        ),
        in_specs=[vmem, vmem],
        out_specs=(vmem,) * 4,
        compiler_params=pltpu.CompilerParams(vmem_limit_bytes=56 * 1024 * 1024),
        name="unpack",
    )(summed, proj)
    g_bias = jnp.concatenate([small[0:64, 0:64], small[0:64, 64:128]], axis=0)
    g_gain = small[64:68].reshape(WIDTH)
    loss = jnp.sum(small[68]) / BATCH
    return (loss, grad_z2, g_qkv, g_out, g_proj, g_bias, g_gain)


def solution(mesh):
    return jax.shard_map(
        on_device,
        mesh=mesh,
        in_specs=(
            P(("dp", "group"), None, None),
            P(("dp", "group"), None, None),
            P(("dp", "group")),
            P(("dp", "group")),
            P(("dp", "group"), None),
            P(),
            P(),
            P(),
            P(),
            P(),
        ),
        out_specs=(P(), P(("dp", "group"), None), P(), P(), P(), P(), P()),
        check_vma=False,
    )
```

time: 1110 us -> 103 us (0.09)
  blocking collectives: 779 us -> 0 us
  waiting for transfers between devices: 171 us -> 0 us
  Pallas kernels: 0 us -> 94.4 us
  matrix products: 54.7 us -> 0 us
  local copies, waits for them, and re-layouts: 51.1 us -> 4.95 us
  other arithmetic: 29.1 us -> 1.3 us
  between operations: 17.1 us -> 2.44 us
    all_gather x1 -> x0, blocking collectives: 629 us -> none  [on_device(): z2_all = lax.all_gather(z2, ('dp', 'group'), axis=0, tiled=True)]
    unnamed x2 -> x0, waiting for transfers between devices: 171 us -> none
    psum x2 -> x0, blocking collectives: 150 us -> none  [the longest x1 75.8 us: on_device(): lax.psum((local_sum, pieces[0].astype(jnp.float32), pieces[1].astype(jnp....]
    pallas_call x0 -> x2, Pallas kernels: none -> 94.4 us  [the longest x1 90.4 us: on_device(): pl.pallas_call(fused, out_shape=(jax.ShapeDtypeStruct((WIDTH, PAYLOAD), B...]
    dot_general x20 -> x0, matrix products: 54.7 us -> none  [the longest x3 13.1 us: encode_core(): jnp.einsum('mihd,mjhd->mhij', query_heads, key_heads, preferred_element_t...]
    reduce_sum x6 -> x1, other arithmetic: 14.5 us -> 1.29 us  [on_device(): loss = jnp.sum(small[68]) / BATCH]
  transfers between devices with their start and end apart: 1 -> 0, of which waited for: 1 -> 0; matrix products, arithmetic and copies ran while one was open for 2% -> 0% of each run, Pallas kernels for 0% -> 0%
where the time goes in v1:
time: 103 us
  Pallas kernels  94.4 us (92%)
  local copies, waits for them, and re-layouts  4.95 us (5%)
  between operations  2.44 us (2%)
  other arithmetic  1.3 us (1%)
    pallas_call x1, Pallas kernels, on_device(): pl.pallas_call(fused, out_shape=(jax.ShapeDtypeStruct((WIDTH, PAYLOAD), B...  90.4 us
    pallas_call x1, Pallas kernels, on_device(): pl.pallas_call(unpack, out_shape=(jax.ShapeDtypeStruct((WIDTH, 3 * WIDTH)...  4.06 us
    unnamed x5, local copies, waits for them, and re-layouts  2.78 us

profile of v1, /device:TPU:1, one launch (start us, length us, event | category | flops | bytes accessed | tf_op | source)
XLA Modules:
  0.0 103.1 jit_solution(148857141150700093)
XLA Ops:
  0.6 1.5 %copy.17.bias_weight = f32[128,64]{1,0:T(8,128)} copy(f32[128,64]{0,1:T(8,128)} %param.18) | data formatting | bytes 65536 | tf_op args[8]
  2.1 90.4 %pretrain_step.1 = (bf16[512,2048]{1,0:T(8,128)(2,1)}, f32[8,128]{1,0:T(8,128)}) custom-call(s32[8]{0:T(128)} %counts.1, s32[8]{0:T(128)} %positives.1, bf16[256,512]{1,0:T(8,128)(2,1)} %bitcast.5, f32[3,8,32]{2,1,0:T(8,128)} %bitcast.6, bf16[8,128]{1,0:T(8,128)(2,1)} %z2.1, bf16[512,1536]{1,0:T(8,128)(2,1)} %wqkv.1, bf16[512,512]{1,0:T(8,128)(2,1)} %wout.1, ...), custom_call_target="tpu_custom_call" | custom-call | tf_op jit(solution)/shard_map/pretrain_step/pallas_call | solution.py:574
  92.5 0.0 copy-start
  92.5 4.1 %unpack.1 = (f32[512,1536]{1,0:T(8,128)}, f32[512,512]{1,0:T(8,128)}, f32[512,128]{1,0:T(8,128)}, f32[80,128]{1,0:T(8,128)}) custom-call(bf16[512,2048]{1,0:T(8,128)(2,1)} %get-tuple-element.13.summed, bf16[512,128]{1,0:T(8,128)(2,1)} %proj.3), custom_call_target="tpu_custom_call" | custom-call | tf_op jit(solution)/shard_map/unpack/pallas_call | solution.py:600
  96.6 1.3 %slice_reduce_fusion = f32[]{:T(128)} fusion(f32[80,128]{1,0:T(8,128)} %get-tuple-element.14), kind=kLoop, calls=%fused_computation.2 | loop fusion | flops 127 | bytes 516 | tf_op jit(solution)/shard_map/reduce_sum | solution.py:615
  98.5 1.3 %slice_bitcast_fusion = f32[512]{0:T(512)} fusion(f32[80,128]{1,0:T(8,128)} %get-tuple-element.14), kind=kLoop, calls=%fused_computation.1 | loop fusion | bytes 4096 | tf_op jit(solution)/shard_map/reshape | solution.py:614
  99.8 0.9 fusion
  100.7 0.7 copy.18
  101.4 0.0 copy-done
  101.4 0.6 copy.20
  (1 shorter events, 0.0 us)
Async XLA Ops:
  92.5 8.9 %copy-start = (f32[8,128]{1,0:T(8,128)S(1)}, f32[8,128]{1,0:T(8,128)}, u32[]{:S(2)}) copy-start(f32[8,128]{1,0:T(8,128)} %get-tuple-element.36) | copy-start | bytes 12292

commit v2 on v1

v2 whole, which is shorter than its diff:
```python
import functools

import jax
import jax.numpy as jnp
from jax import lax
from jax.experimental import pallas as pl
from jax.experimental.pallas import tpu as pltpu
from jax.sharding import PartitionSpec as P

MESH = pl.DeviceIdType.MESH
F32 = jnp.float32
BF = jnp.bfloat16

MOLS = 8
PAIRS = 4
ATOMS = 32
WIDTH = 512
HEADS = 64
HEAD_DIM = 8
KERNELS = 128
LANES = 128
WIDE = HEAD_DIM * LANES
BATCH = 2048
SIDE = 16
DEPTH = 8

VALUE, CTX, HEAD, QUERY, KEY, SMALL, PAYLOAD = 0, 512, 640, 768, 1280, 1792, 1920
CHUNKS = (((0, 384), (384, 768)), ((768, 1152), (1152, 1536)), ((1536, 1792), (1792, 1920)))

Z2, POS, Z3, ROWS, COLS, UNIT, GZ2 = range(7)
FIRST, SECOND, RING, SHARE_SECOND, SHARE_FIRST, CORE_OUT = (7 + 6 * n for n in range(6))
CORE = 43
KINDS = CORE + 3


def mm(a, b):
    return lax.dot_general(a, b, (((1,), (0,)), ((), ())), preferred_element_type=F32)


def mm_t(a, b):
    return lax.dot_general(a, b, (((1,), (1,)), ((), ())), preferred_element_type=F32)


def tmm(a, b):
    return lax.dot_general(a, b, (((0,), (0,)), ((), ())), preferred_element_type=F32)


def halves(values):
    high = values.astype(BF)
    return high, (values - high.astype(F32)).astype(BF)


def stacked(values):
    high = values.astype(BF).astype(F32)
    return jnp.concatenate([high, values - high], axis=0).astype(BF)


def two_part(values, weights, product):
    rows = values.shape[0]
    both = product(stacked(values), weights)
    return both[:rows] + both[rows:]


def lane_is_odd(shape):
    return (lax.broadcasted_iota(jnp.int32, shape, len(shape) - 1) & 64) != 0


def remote(src, dst, sems, kind, device):
    return pltpu.make_async_remote_copy(
        src_ref=src,
        dst_ref=dst,
        send_sem=sems[0].at[kind],
        recv_sem=sems[1].at[kind],
        device_id=device,
        device_id_type=MESH,
    )


def subsets(flips, start):
    places = [start]
    for flip in flips:
        places = places + [tuple(p + f for p, f in zip(place, flip)) for place in places]
    return places


def normalize(feats, counts, gain, s):
    x = feats[...].astype(F32)
    mean = jnp.mean(x, axis=-1, keepdims=True)
    centred = x - mean
    var = jnp.mean(centred * centred, axis=-1, keepdims=True)
    xhat = centred * lax.rsqrt(var + 1e-05)
    s.xhat[...] = xhat
    normed = (xhat * gain[...]).astype(BF)
    s.normed[...] = normed
    for m in range(MOLS):
        valid = lax.broadcasted_iota(jnp.int32, (ATOMS, WIDTH), 0) < counts[m]
        s.xsum[m : m + 1, :] = jnp.sum(
            jnp.where(valid, x[m * ATOMS : (m + 1) * ATOMS], 0.0), axis=0, keepdims=True
        )


def make_perm(s):
    row = lax.broadcasted_iota(jnp.int32, (WIDTH, WIDE), 0)
    col = lax.broadcasted_iota(jnp.int32, (WIDTH, WIDE), 1)
    placed = ((row >> 3) == (col & 63)) & ((row & 7) == (col >> 7))
    s.perm[...] = jnp.where(placed, 1.0, 0.0).astype(BF)


def project(wqkv, s):
    normed = s.normed[...]
    odd = lane_is_odd((ATOMS, WIDE))
    for part, (target, scale) in enumerate(((s.q, HEAD_DIM ** (-0.5)), (s.k, 1.0), (s.v, 1.0))):
        projected = mm(normed, wqkv[:, part * WIDTH : (part + 1) * WIDTH]).astype(BF)
        spread = mm(projected, s.perm[...])
        for p in range(PAIRS):
            low = spread[(2 * p) * ATOMS : (2 * p + 1) * ATOMS]
            high = spread[(2 * p + 1) * ATOMS : (2 * p + 2) * ATOMS]
            merged = jnp.where(odd, high, low)
            target[p] = merged * scale if scale != 1.0 else merged


def distances(coords, s):
    atom = lax.broadcasted_iota(jnp.int32, (ATOMS, ATOMS * ATOMS), 0)
    pair = lax.broadcasted_iota(jnp.int32, (ATOMS, ATOMS * ATOMS), 1)
    select = (
        jnp.where(atom == (pair & 31), 1.0, 0.0) - jnp.where(atom == (pair >> 5), 1.0, 0.0)
    ).astype(BF)
    squared = jnp.zeros((MOLS, ATOMS * ATOMS), F32)
    for c in range(3):
        values = coords[c]
        first = values.astype(BF).astype(F32)
        second = (values - first).astype(BF).astype(F32)
        third = values - first - second
        three = mm(jnp.concatenate([first, second, third], axis=0).astype(BF), select)
        offset = three[:MOLS] + three[MOLS : 2 * MOLS] + three[2 * MOLS :]
        squared = squared + offset * offset
    distance = jnp.sqrt(squared + 0.25)
    for m in range(MOLS):
        s.distance[m] = distance[m : m + 1]


def bias_matrix(bias_t, s):
    turned = jnp.concatenate([bias_t[...], bias_t[...]], axis=0)
    upper = lax.broadcasted_iota(jnp.int32, (LANES, KERNELS), 0) < HEADS
    blocks = jnp.concatenate([jnp.where(upper, turned, 0.0), jnp.where(upper, 0.0, turned)], axis=1)
    s.bias_lhs[...] = stacked(blocks)


def pair_biases(s):
    centers = lax.broadcasted_iota(jnp.int32, (KERNELS, 2 * LANES), 0).astype(F32) * (12.0 / KERNELS)

    def one_pair(p, carry):
        for block in range(4):
            at = pl.ds(block * 256, 256)
            basis = []
            for parity in range(2):
                away = (s.distance[2 * p + parity, :, at] - centers) * 2.0
                basis.append(jnp.exp(-(away * away)))
            high, low = halves(jnp.concatenate(basis, axis=0))
            s.basis[p, :, at] = high
            both = mm(s.bias_lhs[...], high)
            bias = both[:LANES] + both[LANES:] + mm(s.bias_lhs[:LANES, :], low)
            s.attn[p, at, :] = bias.T
        return carry

    lax.fori_loop(0, PAIRS, one_pair, 0)


def attend(counts, s):
    def one_pair(p, carry):
        count = jnp.where(lane_is_odd((1, LANES)), counts[2 * p + 1], counts[2 * p])
        top = jnp.full((ATOMS, LANES), -1e30, F32)
        for j in range(ATOMS):
            at = pl.ds(j * ATOMS, ATOMS)
            score = s.attn[p, at, :]
            for d in range(HEAD_DIM):
                lanes = pl.ds(d * LANES, LANES)
                score = score + s.q[p, :, lanes] * s.k[p, j : j + 1, lanes]
            score = jnp.where(j < count, score, -1e30)
            s.attn[p, at, :] = score
            top = jnp.maximum(top, score)
        total = jnp.zeros((ATOMS, LANES), F32)
        for j in range(ATOMS):
            at = pl.ds(j * ATOMS, ATOMS)
            expo = jnp.exp(s.attn[p, at, :] - top)
            s.attn[p, at, :] = expo
            total = total + expo
        real = lax.broadcasted_iota(jnp.int32, (ATOMS, LANES), 0) < count
        share = jnp.where(real, 1.0 / total, 0.0)
        for j in range(ATOMS):
            at = pl.ds(j * ATOMS, ATOMS)
            weight = s.attn[p, at, :] * share
            s.attn[p, at, :] = weight
            s.column[p, j : j + 1, :] = jnp.sum(weight, axis=0, keepdims=True)
        odd_row = lane_is_odd((1, LANES))
        for d in range(HEAD_DIM):
            lanes = pl.ds(d * LANES, LANES)
            context = jnp.sum(s.column[p] * s.v[p, :, lanes], axis=0, keepdims=True)
            s.context[2 * p, :, lanes] = jnp.where(odd_row, 0.0, context)
            s.context[2 * p + 1, :, lanes] = jnp.where(odd_row, context, 0.0)
        return carry

    lax.fori_loop(0, PAIRS, one_pair, 0)

def pool(wout, proj, s):
    context = jnp.concatenate([s.context[m] for m in range(MOLS)], axis=0)
    context = two_part(context, s.perm[...], mm_t)
    s.ctx_sum[...] = context
    pooled = (s.xsum[...] + two_part(context, wout[...], mm)).astype(BF)
    s.pooled[...] = pooled.astype(F32)
    return mm(pooled, proj[...])


def start_backward(grad_z3, wout, proj, s):
    cs_high, cs_low = halves(s.ctx_sum[...])
    g_high, g_low = halves(grad_z3)
    f = lambda v: v.astype(F32)
    left = jnp.concatenate([f(cs_high), f(cs_low), f(cs_high)], axis=0).astype(BF)
    right = jnp.concatenate([f(g_high), f(g_high), f(g_low)], axis=0).astype(BF)
    s.payload[:, CTX:HEAD] = tmm(left, right).astype(BF)
    left = jnp.concatenate([s.pooled[...], s.pooled[...]], axis=0).astype(BF)
    right = jnp.concatenate([f(g_high), f(g_low)], axis=0).astype(BF)
    s.payload[:, HEAD:QUERY] = tmm(left, right).astype(BF)

    grad_pooled = two_part(grad_z3, proj[...], mm_t)
    grad_ctx = two_part(grad_pooled, wout[...], mm_t)
    spread = two_part(grad_ctx, s.perm[...], mm)
    for m in range(MOLS):
        s.context[m] = spread[m : m + 1]


def value_backward(s):
    odd_row = lane_is_odd((1, LANES))

    def one_pair(p, carry):
        along = jnp.zeros((ATOMS, LANES), F32)
        for d in range(HEAD_DIM):
            lanes = pl.ds(d * LANES, LANES)
            grad = jnp.where(odd_row, s.context[2 * p + 1, :, lanes], s.context[2 * p, :, lanes])
            along = along + grad * s.v[p, :, lanes]
            s.dv[p, :, lanes] = (s.column[p] * grad).astype(BF)
        s.along[p] = along
        return carry

    lax.fori_loop(0, PAIRS, one_pair, 0)


def attend_backward(s):
    scale = HEAD_DIM ** (-0.5)

    def one_pair(p, carry):
        mean = jnp.zeros((ATOMS, LANES), F32)
        for j in range(ATOMS):
            mean = mean + s.attn[p, pl.ds(j * ATOMS, ATOMS), :] * s.along[p, j : j + 1, :]
        for half in range(2):
            ds_range = range(4 * half, 4 * half + 4)
            sums = [jnp.zeros((ATOMS, LANES), F32) for d in ds_range]
            for j in range(ATOMS):
                at = pl.ds(j * ATOMS, ATOMS)
                if half == 0:
                    slope = s.attn[p, at, :] * (s.along[p, j : j + 1, :] - mean)
                    s.attn[p, at, :] = slope
                else:
                    slope = s.attn[p, at, :]
                for n, d in enumerate(ds_range):
                    lanes = pl.ds(d * LANES, LANES)
                    sums[n] = sums[n] + slope * s.k[p, j : j + 1, lanes]
                    s.dk[j : j + 1, lanes] = jnp.sum(slope * s.q[p, :, lanes], axis=0, keepdims=True)
            for n, d in enumerate(ds_range):
                s.dqs[p, :, pl.ds(d * LANES, LANES)] = (sums[n] * scale).astype(BF)
        s.dks[p] = s.dk[...].astype(BF)
        return carry

    lax.fori_loop(0, PAIRS, one_pair, 0)


def bias_backward(s):
    bias_sum = jnp.zeros((2 * KERNELS, LANES), F32)
    for p in range(PAIRS):
        bias_sum = bias_sum + mm(s.basis[p], s.attn[p].astype(BF))
    odd = lane_is_odd((KERNELS, LANES))
    folded = jnp.where(odd, bias_sum[KERNELS:], bias_sum[:KERNELS]).T
    s.small[...] = jnp.zeros((WIDTH, LANES), F32)
    s.small[0:64, :] = folded[:64] + folded[64:]


def project_backward(source, part, target, s):
    odd = lane_is_odd((ATOMS, WIDE))
    zero = jnp.zeros((ATOMS, WIDE), BF)
    pieces = []
    for m in range(MOLS):
        value = source[m // 2]
        pieces.append(jnp.where(odd, value, zero) if m % 2 else jnp.where(odd, zero, value))
    dproj = mm_t(jnp.concatenate(pieces, axis=0), s.perm[...]).astype(BF)
    s.dproj[:, part * WIDTH : (part + 1) * WIDTH] = dproj
    s.payload[:, target : target + WIDTH] = tmm(s.normed[...], dproj).astype(BF)


def gain_backward(wqkv, s):
    grad_normed = mm_t(s.dproj[...], wqkv[...])
    grad_gain = jnp.sum(grad_normed * s.xhat[...], axis=0, keepdims=True)
    for n in range(4):
        s.small[64 + n : 65 + n, :] = grad_gain[:, n * LANES : (n + 1) * LANES]


def fused(
    counts,
    positives,
    feats_in,
    coords,
    z2,
    wqkv_in,
    wout_in,
    proj_in,
    bias_t,
    gain,
    summed_out,
    grad_z2,
    *scratch,
):
    s = Scratch(scratch)
    sems = (s.send, s.recv)
    loads = [
        pltpu.make_async_copy(src, dst, s.load.at[n])
        for n, (src, dst) in enumerate(
            ((feats_in, s.feats), (wqkv_in, s.wqkv), (wout_in, s.wout), (proj_in, s.proj))
        )
    ]
    for load in loads:
        load.start()
    feats, wqkv, wout, proj = s.feats, s.wqkv, s.wout, s.proj

    dp, y_high = lax.axis_index("dp"), lax.axis_index("group")
    bits = [(dp // 2**n) % 2 for n in range(7)]
    cross = [2**n * (1 - 2 * bits[n]) for n in range(7)]
    cross_y = 1 - 2 * y_high
    core = bits[0]
    x_at = bits[1] + 2 * bits[2]
    y_at = bits[3] * 2 + y_high
    ring = dp // 16
    plane = y_high + 2 * x_at + 8 * bits[3]
    depth = core + 2 * ring
    along_row = subsets(
        ((0, cross_y, cross_y), (cross[1], 0, cross[1]), (cross[2], 0, cross[2]), (cross[3], 0, cross[3])),
        (dp, y_high, plane),
    )
    along_col = subsets(
        (
            (cross[0], 0, cross[0]),
            (cross[4], 0, 2 * (1 - 2 * bits[4])),
            (cross[5], 0, 4 * (1 - 2 * bits[5])),
            (cross[6], 0, 8 * (1 - 2 * bits[6])),
        ),
        (dp, y_high, depth),
    )
    along_x = subsets(
        ((cross[1], 0, 1 - 2 * bits[1]), (cross[2], 0, 2 * (1 - 2 * bits[2]))), (dp, y_high, x_at)
    )
    along_y = subsets(
        ((0, cross_y, cross_y), (cross[3], 0, 2 * (1 - 2 * bits[3]))), (dp, y_high, y_at)
    )
    along_ring = along_col[0::2]
    sibling = along_col[1][:2]

    barrier = pltpu.get_barrier_semaphore()
    for place in along_row[1:] + along_col[1:]:
        pl.semaphore_signal(barrier, inc=1, device_id=place[:2], device_id_type=MESH)

    loads[0].wait()
    normalize(feats, counts, gain, s)
    make_perm(s)
    loads[1].wait()
    project(wqkv, s)
    pl.semaphore_wait(barrier, 2 * (SIDE - 1))

    def slot(n):
        return pl.ds(n * 8, 8)

    others = range(1, SIDE)

    def start(copy, offsets=others):
        for o in offsets:
            copy(o).start()

    def all_of(ref, kind):
        return remote(ref, ref, sems, kind, sibling)

    def wait(ref, kind):
        all_of(ref, kind).wait()

    s.z2[slot(depth), :] = z2[...].astype(F32)
    targets = jnp.zeros((8, LANES), jnp.int32)
    sub = lax.broadcasted_iota(jnp.int32, (8, LANES), 0)
    for n in range(8):
        targets = jnp.where(sub == n, positives[n], targets)
    s.pos[slot(plane), :] = targets

    def z2_copy(o):
        mine = s.z2.at[slot(depth), :]
        return remote(mine, mine, sems, Z2, along_col[o][:2])

    def pos_copy(o):
        mine = s.pos.at[slot(plane), :]
        return remote(mine, mine, sems, POS, along_row[o][:2])

    def z3_copy(o):
        mine = s.z3.at[slot(plane), :]
        return remote(mine, mine, sems, Z3, along_row[o][:2])

    def rows_copy(o):
        mine = s.rows.at[plane]
        return remote(mine, mine, sems, ROWS, along_row[o][:2])

    def cols_copy(o):
        mine = s.cols.at[depth]
        return remote(mine, mine, sems, COLS, along_col[o][:2])

    def unit_copy(o):
        peer = along_row[o]
        return remote(s.unit.at[peer[2]], s.unit_in.at[plane], sems, UNIT, peer[:2])

    def gz2_copy(o):
        peer = along_col[o]
        return remote(s.gz2.at[peer[2]], s.gz2_in.at[depth], sems, GZ2, peer[:2])

    start(z2_copy)
    start(pos_copy)

    distances(coords, s)
    bias_matrix(bias_t, s)
    pair_biases(s)
    attend(counts, s)
    loads[2].wait()
    loads[3].wait()
    z3 = pool(wout, proj, s)
    inverse = lax.rsqrt(jnp.mean(z3 * z3, axis=1, keepdims=True) + 1e-06) * LANES ** (-0.5)
    s.z3[slot(plane), :] = (z3 * inverse).astype(BF).astype(F32)
    start(z3_copy)
    wait(s.z2.at[pl.ds(0, 120), :], Z2)
    wait(s.pos.at[pl.ds(0, 120), :], POS)
    wait(s.z3.at[pl.ds(0, 120), :], Z3)

    z3_all = s.z3[...].astype(BF)
    z2_all = s.z2[...].astype(BF)
    logits = mm_t(z3_all, z2_all)
    expo = jnp.exp(logits)
    expo_t = jnp.exp(mm_t(z2_all, z3_all))
    s.rows[plane] = jnp.broadcast_to(jnp.sum(expo_t, axis=0, keepdims=True), (8, LANES))
    s.cols[depth] = jnp.broadcast_to(jnp.sum(expo, axis=0, keepdims=True), (8, LANES))
    start(rows_copy)
    start(cols_copy)
    lane = lax.broadcasted_iota(jnp.int32, (LANES, LANES), 1)
    owner = (lane >> 4) * 32 + ((lane >> 3) & 1) * 2 + (dp * 2 + y_high - ring * 32 - core * 2)
    column_id = owner * 8 + (lane & 7)
    hit = s.pos[...] == column_id
    score = jnp.sum(jnp.where(hit, logits, 0.0), axis=0, keepdims=True)
    wait(s.rows.at[pl.ds(0, 15)], ROWS)
    wait(s.cols.at[pl.ds(0, 15)], COLS)
    row_sum = s.rows[0]
    col_sum = s.cols[0]
    for n in range(1, SIDE):
        row_sum = row_sum + s.rows[n]
        col_sum = col_sum + s.cols[n]
    row_half = jnp.broadcast_to(0.5 / row_sum[0:1], (LANES, LANES)).T
    slope = expo * (row_half + 0.5 / col_sum[0:1]) - jnp.where(hit, 1.0, 0.0)
    unit = mm(slope.astype(BF), z2_all)
    for n in range(SIDE):
        s.unit[n] = unit[n * 8 : (n + 1) * 8]
    s.unit_in[plane] = s.unit[plane]
    start(unit_copy)
    grad_cols = tmm(slope.astype(BF), z3_all)
    for n in range(SIDE):
        s.gz2[n] = grad_cols[n * 8 : (n + 1) * 8]
    s.gz2_in[depth] = s.gz2[depth]
    start(gz2_copy)
    one_lane = lax.broadcasted_iota(jnp.int32, (1, LANES), 1)
    row_term = jnp.where((one_lane >> 3) == plane, 0.5 * jnp.log(row_sum[0:1]), 0.0)
    col_term = jnp.where((one_lane >> 3) == depth, 0.5 * jnp.log(col_sum[0:1]), 0.0)
    loss_terms = row_term + col_term - score

    wait(s.unit_in.at[pl.ds(0, 15)], UNIT)
    grad_unit = s.unit_in[0]
    for n in range(1, SIDE):
        grad_unit = grad_unit + s.unit_in[n]
    dot = jnp.sum(z3 * grad_unit, axis=1, keepdims=True)
    grad_z3 = inverse * (grad_unit - z3 * dot * (inverse * inverse))

    summed = s.summed
    ways = ((along_x, x_at, along_y, y_at), (along_y, y_at, along_x, x_at))

    def lanes_of(c, h):
        return pl.ds(CHUNKS[c][h][0], CHUNKS[c][h][1] - CHUNKS[c][h][0])

    def whole(c):
        return pl.ds(CHUNKS[c][0][0], CHUNKS[c][1][1] - CHUNKS[c][0][0])

    def core_copy(c):
        theirs = s.payload.at[pl.ds((1 - core) * 256, 256), whole(c)]
        return remote(theirs, s.core_in.at[:, whole(c)], sems, CORE + c, sibling)

    def first_copy(c, h, o):
        peer, lanes = ways[h][0][o], lanes_of(c, h)
        return remote(
            s.first_out.at[pl.ds(peer[2] * 64, 64), lanes],
            s.first_in.at[ways[h][1], :, lanes],
            sems,
            FIRST + 2 * c + h,
            peer[:2],
        )

    def second_copy(c, h, o):
        peer, lanes = ways[h][2][o], lanes_of(c, h)
        return remote(
            s.second_out.at[pl.ds(peer[2] * 16, 16), lanes],
            s.second_in.at[ways[h][3], :, lanes],
            sems,
            SECOND + 2 * c + h,
            peer[:2],
        )

    def ring_copy(c, h, o):
        lanes = lanes_of(c, h)
        return remote(
            s.ring_out.at[:, lanes],
            s.ring_in.at[ring, :, lanes],
            sems,
            RING + 2 * c + h,
            along_ring[o][:2],
        )

    def second_share(c, h, o):
        mine = summed.at[pl.ds(core * 256 + ways[h][1] * 64 + ways[h][3] * 16, 16), lanes_of(c, h)]
        return remote(mine, mine, sems, SHARE_SECOND + 2 * c + h, ways[h][2][o][:2])

    def first_share(c, h, o):
        mine = summed.at[pl.ds(core * 256 + ways[h][1] * 64, 64), lanes_of(c, h)]
        return remote(mine, mine, sems, SHARE_FIRST + 2 * c + h, ways[h][0][o][:2])

    def core_share(c, h):
        mine = summed.at[pl.ds(core * 256, 256), lanes_of(c, h)]
        return remote(mine, mine, sems, CORE_OUT + 2 * c + h, sibling)

    def store_copy(c):
        return pltpu.make_async_copy(
            summed.at[:, whole(c)], summed_out.at[:, whole(c)], s.load.at[4 + c]
        )

    near, far = range(1, 4), range(1, DEPTH)

    def all_first(c, h):
        return all_of(s.first_in.at[pl.ds(0, 3), :, lanes_of(c, h)], FIRST + 2 * c + h)

    def all_second(c, h):
        return all_of(s.second_in.at[pl.ds(0, 3), :, lanes_of(c, h)], SECOND + 2 * c + h)

    def all_ring(c, h):
        return all_of(s.ring_in.at[pl.ds(0, 7), :, lanes_of(c, h)], RING + 2 * c + h)

    def all_second_share(c, h):
        return all_of(s.second_in.at[pl.ds(0, 3), :, lanes_of(c, h)], SHARE_SECOND + 2 * c + h)

    def all_first_share(c, h):
        return all_of(s.first_in.at[pl.ds(0, 3), :, lanes_of(c, h)], SHARE_FIRST + 2 * c + h)

    def added(ref, count, lanes):
        total = ref[0, :, lanes].astype(F32)
        for n in range(1, count):
            total = total + ref[n, :, lanes].astype(F32)
        return total.astype(BF)

    def first_step(c):
        core_copy(c).wait_recv()
        mine = s.payload[pl.ds(core * 256, 256), whole(c)].astype(F32)
        s.first_out[:, whole(c)] = (mine + s.core_in[:, whole(c)].astype(F32)).astype(BF)
        for h in range(2):
            for o in near:
                first_copy(c, h, o).start()
        for h in range(2):
            lanes, at = lanes_of(c, h), ways[h][1]
            s.first_in[at, :, lanes] = s.first_out[pl.ds(at * 64, 64), lanes]

    def second_step(c):
        for h in range(2):
            lanes, at = lanes_of(c, h), ways[h][3]
            all_first(c, h).wait_recv()
            s.second_out[:, lanes] = added(s.first_in, 4, lanes)
            for o in near:
                second_copy(c, h, o).start()
            s.second_in[at, :, lanes] = s.second_out[pl.ds(at * 16, 16), lanes]

    def ring_step(c):
        for h in range(2):
            lanes = lanes_of(c, h)
            all_second(c, h).wait_recv()
            total = added(s.second_in, 4, lanes)
            s.ring_out[:, lanes] = total
            for o in far:
                ring_copy(c, h, o).start()
            s.ring_in[ring, :, lanes] = total

    def share_second_step(c):
        for h in range(2):
            lanes = lanes_of(c, h)
            all_ring(c, h).wait_recv()
            at = pl.ds(core * 256 + ways[h][1] * 64 + ways[h][3] * 16, 16)
            summed[at, lanes] = added(s.ring_in, DEPTH, lanes)
            for o in near:
                second_share(c, h, o).start()

    def share_first_step(c):
        for h in range(2):
            all_second_share(c, h).wait_recv()
            for o in near:
                first_share(c, h, o).start()

    def share_core_step(c):
        for h in range(2):
            all_first_share(c, h).wait_recv()
            core_share(c, h).start()

    def store_step(c):
        for h in range(2):
            core_share(c, h).wait_recv()
        store_copy(c).start()

    start_backward(grad_z3, wout, proj, s)
    value_backward(s)
    project_backward(s.dv, 2, VALUE, s)
    core_copy(0).start()
    attend_backward(s)
    first_step(0)
    project_backward(s.dqs, 0, QUERY, s)
    project_backward(s.dks, 1, KEY, s)
    core_copy(1).start()
    bias_backward(s)
    second_step(0)
    first_step(1)
    gain_backward(wqkv, s)
    s.small[68:69, :] = loss_terms
    s.payload[:, SMALL:PAYLOAD] = s.small[...].astype(BF)
    core_copy(2).start()
    ring_step(0)
    first_step(2)
    second_step(1)
    second_step(2)
    ring_step(1)
    share_second_step(0)
    ring_step(2)
    share_first_step(0)
    share_second_step(1)
    share_core_step(0)
    share_first_step(1)
    share_second_step(2)
    store_step(0)
    share_core_step(1)
    share_first_step(2)
    store_step(1)
    share_core_step(2)

    wait(s.gz2_in.at[pl.ds(0, 15)], GZ2)
    total = s.gz2_in[0]
    for n in range(1, SIDE):
        total = total + s.gz2_in[n]
    grad_z2[...] = total
    store_step(2)
    for c in range(3):
        core_copy(c).wait_send()
        for h in range(2):
            for group in (all_first, all_second, all_ring, all_second_share, all_first_share):
                group(c, h).wait_send()
            core_share(c, h).wait_send()
    for c in range(3):
        store_copy(c).wait()


SHAPES = {
    "xhat": ((256, WIDTH), F32),
    "normed": ((256, WIDTH), BF),
    "xsum": ((MOLS, WIDTH), F32),
    "perm": ((WIDTH, WIDE), BF),
    "q": ((PAIRS, ATOMS, WIDE), F32),
    "k": ((PAIRS, ATOMS, WIDE), F32),
    "v": ((PAIRS, ATOMS, WIDE), F32),
    "distance": ((MOLS, 1, ATOMS * ATOMS), F32),
    "bias_lhs": ((2 * LANES, 2 * KERNELS), BF),
    "basis": ((PAIRS, 2 * KERNELS, ATOMS * ATOMS), BF),
    "attn": ((PAIRS, ATOMS * ATOMS, LANES), F32),
    "column": ((PAIRS, ATOMS, LANES), F32),
    "context": ((MOLS, 1, WIDE), F32),
    "ctx_sum": ((MOLS, WIDTH), F32),
    "pooled": ((MOLS, WIDTH), F32),
    "along": ((PAIRS, ATOMS, LANES), F32),
    "dk": ((ATOMS, WIDE), F32),
    "dqs": ((PAIRS, ATOMS, WIDE), BF),
    "dks": ((PAIRS, ATOMS, WIDE), BF),
    "dv": ((PAIRS, ATOMS, WIDE), BF),
    "dproj": ((256, 3 * WIDTH), BF),
    "small": ((WIDTH, LANES), F32),
    "payload": ((WIDTH, PAYLOAD), BF),
    "z2": ((LANES, LANES), F32),
    "pos": ((LANES, LANES), jnp.int32),
    "z3": ((LANES, LANES), F32),
    "rows": ((SIDE, 8, LANES), F32),
    "cols": ((SIDE, 8, LANES), F32),
    "unit": ((SIDE, 8, LANES), F32),
    "unit_in": ((SIDE, 8, LANES), F32),
    "gz2": ((SIDE, 8, LANES), F32),
    "gz2_in": ((SIDE, 8, LANES), F32),
    "core_in": ((256, PAYLOAD), BF),
    "first_out": ((256, PAYLOAD), BF),
    "first_in": ((4, 64, PAYLOAD), BF),
    "second_out": ((64, PAYLOAD), BF),
    "second_in": ((4, 16, PAYLOAD), BF),
    "ring_out": ((16, PAYLOAD), BF),
    "ring_in": ((DEPTH, 16, PAYLOAD), BF),
    "summed": ((WIDTH, PAYLOAD), BF),
    "feats": ((256, WIDTH), BF),
    "wqkv": ((WIDTH, 3 * WIDTH), BF),
    "wout": ((WIDTH, WIDTH), BF),
    "proj": ((WIDTH, LANES), BF),
}


class Scratch:
    def __init__(self, refs):
        for name, ref in zip(list(SHAPES) + ["send", "recv", "load"], refs):
            setattr(self, name, ref)


def unpack(summed, proj, cols_in, loss, cols_out, g_qkv, g_out, g_proj, g_bias, g_gain):
    for part, start in enumerate((QUERY, KEY, VALUE)):
        g_qkv[:, part * WIDTH : (part + 1) * WIDTH] = summed[:, start : start + WIDTH].astype(F32)
    g_out[...] = mm_t(summed[:, CTX:HEAD], proj[...])
    g_proj[...] = summed[:, HEAD:QUERY].astype(F32)
    cols_out[...] = cols_in[...]
    g_bias[...] = summed[0:64, SMALL:PAYLOAD].astype(F32)
    small = summed[64:80, SMALL:PAYLOAD].astype(F32)
    for n in range(4):
        g_gain[:, n * LANES : (n + 1) * LANES] = small[n : n + 1]
    loss[...] = jnp.sum(small[4:5], axis=1, keepdims=True) / BATCH


def on_device(
    atom_feats, coords, atom_counts, positives, z2, w_qkv, w_out, proj, bias_weight, ln_gain
):
    vmem = pl.BlockSpec(memory_space=pltpu.VMEM)
    smem = pl.BlockSpec(memory_space=pltpu.SMEM)
    hbm = pl.BlockSpec(memory_space=pl.ANY)
    summed, grad_z2 = pl.pallas_call(
        fused,
        out_shape=(
            jax.ShapeDtypeStruct((WIDTH, PAYLOAD), BF),
            jax.ShapeDtypeStruct((8, LANES), F32),
        ),
        in_specs=[smem, smem, hbm, vmem, vmem, hbm, hbm, hbm, vmem, vmem],
        out_specs=(hbm, vmem),
        scratch_shapes=[pltpu.VMEM(*shape) for shape in SHAPES.values()]
        + [pltpu.SemaphoreType.DMA((KINDS,))] * 2
        + [pltpu.SemaphoreType.DMA((7,))],
        compiler_params=pltpu.CompilerParams(
            collective_id=0, has_side_effects=True, vmem_limit_bytes=56 * 1024 * 1024
        ),
        name="pretrain_step",
    )(
        atom_counts,
        positives,
        atom_feats.reshape(256, WIDTH),
        coords.transpose(1, 0, 2),
        z2,
        w_qkv,
        w_out,
        proj,
        bias_weight.T,
        ln_gain.reshape(1, WIDTH),
    )
    shapes = ((1, 1), (8, LANES), (WIDTH, 3 * WIDTH), (WIDTH, WIDTH), (WIDTH, LANES), (HEADS, KERNELS), (1, WIDTH))
    loss, grad_z2, g_qkv, g_out, g_proj, g_bias, g_gain = pl.pallas_call(
        unpack,
        out_shape=tuple(jax.ShapeDtypeStruct(shape, F32) for shape in shapes),
        in_specs=[vmem] * 3,
        out_specs=(vmem,) * 7,
        compiler_params=pltpu.CompilerParams(vmem_limit_bytes=56 * 1024 * 1024),
        name="unpack",
    )(summed, proj, grad_z2)
    return (loss.reshape(()), grad_z2, g_qkv, g_out, g_proj, g_bias.T, g_gain.reshape(WIDTH))


def solution(mesh):
    return jax.shard_map(
        on_device,
        mesh=mesh,
        in_specs=(
            P(("dp", "group"), None, None),
            P(("dp", "group"), None, None),
            P(("dp", "group")),
            P(("dp", "group")),
            P(("dp", "group"), None),
            P(),
            P(),
            P(),
            P(),
            P(),
        ),
        out_specs=(P(), P(("dp", "group"), None), P(), P(), P(), P(), P()),
        check_vma=False,
    )
```

time: 103 us -> 78.1 us (0.76)
  Pallas kernels: 94.4 us -> 77.3 us
  local copies, waits for them, and re-layouts: 4.95 us -> 0 us
  between operations: 2.44 us -> 0.64 us
  other arithmetic: 1.3 us -> 0 us
    pallas_call x1, Pallas kernels: 90.4 us -> 73.2 us  [on_device(): pl.pallas_call(fused, out_shape=(jax.ShapeDtypeStruct((WIDTH, PAYLOAD), B...]
    unnamed x5 -> x0, local copies, waits for them, and re-layouts: 2.78 us -> none
    reduce_sum x1 -> x0, other arithmetic: 1.29 us -> none  [on_device(): loss = jnp.sum(small[68]) / BATCH]
    reshape x1 -> x0, local copies, waits for them, and re-layouts: 1.26 us -> none  [on_device(): g_gain = small[64:68].reshape(WIDTH)]
where the time goes in v2:
time: 78.1 us; the launch traced here: 77.9 us
  Pallas kernels  77.3 us (99%)
    pallas_call x1, Pallas kernels, on_device(): pl.pallas_call(fused, out_shape=(jax.ShapeDtypeStruct((WIDTH, PAYLOAD), B...  73.2 us
    pallas_call x1, Pallas kernels, on_device(): pl.pallas_call(unpack, out_shape=tuple((jax.ShapeDtypeStruct(shape, F32)...  4.1 us

profile of v2, /device:TPU:1, one launch (start us, length us, event | category | flops | bytes accessed | tf_op | source)
XLA Modules:
  0.0 77.9 jit_solution(5058659615203556911)
XLA Ops:
  0.6 73.2 %pretrain_step.1 = (bf16[512,1920]{1,0:T(8,128)(2,1)}, f32[8,128]{1,0:T(8,128)}) custom-call(s32[8]{0:T(128)} %counts.1, s32[8]{0:T(128)} %positives.1, bf16[256,512]{1,0:T(8,128)(2,1)} %bitcast.7, f32[3,8,32]{2,1,0:T(8,128)} %bitcast.9, bf16[8,128]{1,0:T(8,128)(2,1)} %z2.1, bf16[512,1536]{1,0:T(8,128)(2,1)} %wqkv_in.1, bf16[512,512]{1,0:T(8,128)(2,1)} %wout_in.1, ...), custom_call_target="tpu_custom_call" | custom-call | tf_op jit(solution)/shard_map/pretrain_step/pallas_call | solution.py:749
  73.8 4.1 %unpack.1 = (f32[1,1]{1,0:T(1,128)}, f32[8,128]{1,0:T(8,128)}, f32[512,1536]{1,0:T(8,128)}, f32[512,512]{1,0:T(8,128)}, f32[512,128]{1,0:T(8,128)}, /*index=5*/f32[64,128]{1,0:T(8,128)}, f32[1,512]{1,0:T(1,128)}) custom-call(bf16[512,1920]{1,0:T(8,128)(2,1)} %get-tuple-element.16.summed, bf16[512,128]{1,0:T(8,128)(2,1)} %proj.1, ...), custom_call_target="tpu_custom_call" | custom-call | tf_op jit(solution)/shard_map/unpack/pallas_call | solution.py:777

commit v3 on v2

--- a/solution.py
+++ b/solution.py
@@ -163,7 +163,7 @@
             s.attn[p, at, :] = bias.T
         return carry
 
-    lax.fori_loop(0, PAIRS, one_pair, 0)
+    lax.fori_loop(0, PAIRS, one_pair, 0, unroll=True)
 
 
 def attend(counts, s):
@@ -200,7 +200,7 @@
             s.context[2 * p + 1, :, lanes] = jnp.where(odd_row, context, 0.0)
         return carry
 
-    lax.fori_loop(0, PAIRS, one_pair, 0)
+    lax.fori_loop(0, PAIRS, one_pair, 0, unroll=True)
 
 def pool(wout, proj, s):
     context = jnp.concatenate([s.context[m] for m in range(MOLS)], axis=0)
@@ -242,10 +242,10 @@
         s.along[p] = along
         return carry
 
-    lax.fori_loop(0, PAIRS, one_pair, 0)
-
-
-def attend_backward(s):
+    lax.fori_loop(0, PAIRS, one_pair, 0, unroll=True)
+
+
+def attend_backward(first, last, s):
     scale = HEAD_DIM ** (-0.5)
 
     def one_pair(p, carry):
@@ -271,7 +271,7 @@
         s.dks[p] = s.dk[...].astype(BF)
         return carry
 
-    lax.fori_loop(0, PAIRS, one_pair, 0)
+    lax.fori_loop(first, last, one_pair, 0, unroll=True)
 
 
 def bias_backward(s):
@@ -314,8 +314,9 @@
     proj_in,
     bias_t,
     gain,
-    summed_out,
+    summed,
     grad_z2,
+    proj,
     *scratch,
 ):
     s = Scratch(scratch)
@@ -323,12 +324,12 @@
     loads = [
         pltpu.make_async_copy(src, dst, s.load.at[n])
         for n, (src, dst) in enumerate(
-            ((feats_in, s.feats), (wqkv_in, s.wqkv), (wout_in, s.wout), (proj_in, s.proj))
+            ((feats_in, s.feats), (wqkv_in, s.wqkv), (wout_in, s.wout), (proj_in, proj))
         )
     ]
     for load in loads:
         load.start()
-    feats, wqkv, wout, proj = s.feats, s.wqkv, s.wout, s.proj
+    feats, wqkv, wout = s.feats, s.wqkv, s.wout
 
     dp, y_high = lax.axis_index("dp"), lax.axis_index("group")
     bits = [(dp // 2**n) % 2 for n in range(7)]
@@ -371,6 +372,9 @@
     make_perm(s)
     loads[1].wait()
     project(wqkv, s)
+    distances(coords, s)
+    bias_matrix(bias_t, s)
+    pair_biases(s)
     pl.semaphore_wait(barrier, 2 * (SIDE - 1))
 
     def slot(n):
@@ -426,9 +430,6 @@
     start(z2_copy)
     start(pos_copy)
 
-    distances(coords, s)
-    bias_matrix(bias_t, s)
-    pair_biases(s)
     attend(counts, s)
     loads[2].wait()
     loads[3].wait()
@@ -485,7 +486,6 @@
     dot = jnp.sum(z3 * grad_unit, axis=1, keepdims=True)
     grad_z3 = inverse * (grad_unit - z3 * dot * (inverse * inverse))
 
-    summed = s.summed
     ways = ((along_x, x_at, along_y, y_at), (along_y, y_at, along_x, x_at))
 
     def lanes_of(c, h):
@@ -539,11 +539,6 @@
     def core_share(c, h):
         mine = summed.at[pl.ds(core * 256, 256), lanes_of(c, h)]
         return remote(mine, mine, sems, CORE_OUT + 2 * c + h, sibling)
-
-    def store_copy(c):
-        return pltpu.make_async_copy(
-            summed.at[:, whole(c)], summed_out.at[:, whole(c)], s.load.at[4 + c]
-        )
 
     near, far = range(1, 4), range(1, DEPTH)
 
@@ -618,59 +613,57 @@
             all_first_share(c, h).wait_recv()
             core_share(c, h).start()
 
-    def store_step(c):
+    def arrive_step(c):
         for h in range(2):
             core_share(c, h).wait_recv()
-        store_copy(c).start()
 
     start_backward(grad_z3, wout, proj, s)
     value_backward(s)
     project_backward(s.dv, 2, VALUE, s)
     core_copy(0).start()
-    attend_backward(s)
+    attend_backward(0, 2, s)
     first_step(0)
+    attend_backward(2, PAIRS, s)
     project_backward(s.dqs, 0, QUERY, s)
     project_backward(s.dks, 1, KEY, s)
     core_copy(1).start()
     bias_backward(s)
-    second_step(0)
     first_step(1)
     gain_backward(wqkv, s)
     s.small[68:69, :] = loss_terms
     s.payload[:, SMALL:PAYLOAD] = s.small[...].astype(BF)
     core_copy(2).start()
+    second_step(0)
+    first_step(2)
     ring_step(0)
-    first_step(2)
     second_step(1)
     second_step(2)
     ring_step(1)
+    ring_step(2)
     share_second_step(0)
-    ring_step(2)
     share_first_step(0)
     share_second_step(1)
+    share_second_step(2)
+    share_first_step(1)
     share_core_step(0)
-    share_first_step(1)
-    share_second_step(2)
-    store_step(0)
+    share_first_step(2)
     share_core_step(1)
-    share_first_step(2)
-    store_step(1)
+    arrive_step(0)
     share_core_step(2)
+    arrive_step(1)
 
     wait(s.gz2_in.at[pl.ds(0, 15)], GZ2)
     total = s.gz2_in[0]
     for n in range(1, SIDE):
         total = total + s.gz2_in[n]
     grad_z2[...] = total
-    store_step(2)
+    arrive_step(2)
     for c in range(3):
         core_copy(c).wait_send()
         for h in range(2):
             for group in (all_first, all_second, all_ring, all_second_share, all_first_share):
                 group(c, h).wait_send()
             core_share(c, h).wait_send()
-    for c in range(3):
-        store_copy(c).wait()
 
 
 SHAPES = {
@@ -713,11 +706,9 @@
     "second_in": ((4, 16, PAYLOAD), BF),
     "ring_out": ((16, PAYLOAD), BF),
     "ring_in": ((DEPTH, 16, PAYLOAD), BF),
-    "summed": ((WIDTH, PAYLOAD), BF),
     "feats": ((256, WIDTH), BF),
     "wqkv": ((WIDTH, 3 * WIDTH), BF),
     "wout": ((WIDTH, WIDTH), BF),
-    "proj": ((WIDTH, LANES), BF),
 }
 
 
@@ -727,17 +718,34 @@
             setattr(self, name, ref)
 
 
-def unpack(summed, proj, cols_in, loss, cols_out, g_qkv, g_out, g_proj, g_bias, g_gain):
-    for part, start in enumerate((QUERY, KEY, VALUE)):
-        g_qkv[:, part * WIDTH : (part + 1) * WIDTH] = summed[:, start : start + WIDTH].astype(F32)
-    g_out[...] = mm_t(summed[:, CTX:HEAD], proj[...])
-    g_proj[...] = summed[:, HEAD:QUERY].astype(F32)
+def unpack(
+    summed, cols_in, proj, loss, cols_out, g_qkv, g_out, g_proj, g_bias, g_gain, qkv, out, head, sems
+):
+    copies = []
+
+    def store(src, dst):
+        copies.append(pltpu.make_async_copy(src, dst, sems.at[len(copies)]))
+        copies[-1].start()
+
+    for n in range(4):
+        at = pl.ds(n * 128, 128)
+        for part, start in enumerate((QUERY, KEY, VALUE)):
+            qkv[at, part * WIDTH : (part + 1) * WIDTH] = summed[at, start : start + WIDTH].astype(F32)
+        store(qkv.at[at, :], g_qkv.at[at, :])
+    for n in range(2):
+        at = pl.ds(n * 256, 256)
+        out[at, :] = mm_t(summed[at, CTX:HEAD], proj[...])
+        store(out.at[at, :], g_out.at[at, :])
+    head[...] = summed[:, HEAD:QUERY].astype(F32)
+    store(head, g_proj)
     cols_out[...] = cols_in[...]
     g_bias[...] = summed[0:64, SMALL:PAYLOAD].astype(F32)
     small = summed[64:80, SMALL:PAYLOAD].astype(F32)
     for n in range(4):
         g_gain[:, n * LANES : (n + 1) * LANES] = small[n : n + 1]
     loss[...] = jnp.sum(small[4:5], axis=1, keepdims=True) / BATCH
+    for copy in copies:
+        copy.wait()
 
 
 def on_device(
@@ -746,17 +754,18 @@
     vmem = pl.BlockSpec(memory_space=pltpu.VMEM)
     smem = pl.BlockSpec(memory_space=pltpu.SMEM)
     hbm = pl.BlockSpec(memory_space=pl.ANY)
-    summed, grad_z2 = pl.pallas_call(
+    summed, grad_z2, proj_near = pl.pallas_call(
         fused,
         out_shape=(
-            jax.ShapeDtypeStruct((WIDTH, PAYLOAD), BF),
-            jax.ShapeDtypeStruct((8, LANES), F32),
+            pltpu.VMEM((WIDTH, PAYLOAD), BF),
+            pltpu.VMEM((8, LANES), F32),
+            pltpu.VMEM((WIDTH, LANES), BF),
         ),
         in_specs=[smem, smem, hbm, vmem, vmem, hbm, hbm, hbm, vmem, vmem],
-        out_specs=(hbm, vmem),
+        out_specs=(vmem, vmem, vmem),
         scratch_shapes=[pltpu.VMEM(*shape) for shape in SHAPES.values()]
         + [pltpu.SemaphoreType.DMA((KINDS,))] * 2
-        + [pltpu.SemaphoreType.DMA((7,))],
+        + [pltpu.SemaphoreType.DMA((4,))],
         compiler_params=pltpu.CompilerParams(
             collective_id=0, has_side_effects=True, vmem_limit_bytes=56 * 1024 * 1024
         ),
@@ -777,11 +786,17 @@
     loss, grad_z2, g_qkv, g_out, g_proj, g_bias, g_gain = pl.pallas_call(
         unpack,
         out_shape=tuple(jax.ShapeDtypeStruct(shape, F32) for shape in shapes),
-        in_specs=[vmem] * 3,
-        out_specs=(vmem,) * 7,
-        compiler_params=pltpu.CompilerParams(vmem_limit_bytes=56 * 1024 * 1024),
+        in_specs=[vmem, vmem, vmem],
+        out_specs=(vmem, vmem, hbm, hbm, hbm, vmem, vmem),
+        scratch_shapes=[
+            pltpu.VMEM((WIDTH, 3 * WIDTH), F32),
+            pltpu.VMEM((WIDTH, WIDTH), F32),
+            pltpu.VMEM((WIDTH, LANES), F32),
+            pltpu.SemaphoreType.DMA((7,)),
+        ],
+        compiler_params=pltpu.CompilerParams(vmem_limit_bytes=32 * 1024 * 1024),
         name="unpack",
-    )(summed, proj, grad_z2)
+    )(summed, grad_z2, proj_near)
     return (loss.reshape(()), grad_z2, g_qkv, g_out, g_proj, g_bias.T, g_gain.reshape(WIDTH))
 
 

time: 78.1 us -> 75.3 us (0.964)
  Pallas kernels: 77.3 us -> 74.3 us
    pallas_call x1, Pallas kernels: 73.2 us -> 71.3 us  [on_device(): pl.pallas_call(fused, out_shape=(pltpu.VMEM((WIDTH, PAYLOAD), BF), pltpu....]
    pallas_call x1, Pallas kernels: 4.1 us -> 2.97 us  [on_device(): pl.pallas_call(unpack, out_shape=tuple((jax.ShapeDtypeStruct(shape, F32)...]
where the time goes in v3:
time: 75.3 us; the launch traced here: 75.1 us
  Pallas kernels  74.3 us (99%)
  between operations  0.8 us (1%)
    pallas_call x1, Pallas kernels, on_device(): pl.pallas_call(fused, out_shape=(pltpu.VMEM((WIDTH, PAYLOAD), BF), pltpu....  71.3 us
    pallas_call x1, Pallas kernels, on_device(): pl.pallas_call(unpack, out_shape=tuple((jax.ShapeDtypeStruct(shape, F32)...  2.97 us

profile of v3, /device:TPU:1, one launch (start us, length us, event | category | flops | bytes accessed | tf_op | source)
XLA Modules:
  0.0 75.1 jit_solution(10273613329455893397)
XLA Ops:
  0.6 71.3 %pretrain_step.1 = (bf16[512,1920]{1,0:T(8,128)(2,1)S(1)}, f32[8,128]{1,0:T(8,128)S(1)}, bf16[512,128]{1,0:T(8,128)(2,1)S(1)}) custom-call(s32[8]{0:T(128)} %counts.1, s32[8]{0:T(128)} %positives.1, bf16[256,512]{1,0:T(8,128)(2,1)} %bitcast.7, f32[3,8,32]{2,1,0:T(8,128)} %bitcast.9, bf16[8,128]{1,0:T(8,128)(2,1)} %z2.1, bf16[512,1536]{1,0:T(8,128)(2,1)} %wqkv_in.1, ...), custom_call_target="tpu_custom_call" | custom-call | tf_op jit(solution)/shard_map/pretrain_step/pallas_call | solution.py:757
  71.9 3.0 %unpack.1 = (f32[1,1]{1,0:T(1,128)}, f32[8,128]{1,0:T(8,128)}, f32[512,1536]{1,0:T(8,128)}, f32[512,512]{1,0:T(8,128)}, f32[512,128]{1,0:T(8,128)}, /*index=5*/f32[64,128]{1,0:T(8,128)}, f32[1,512]{1,0:T(1,128)}) custom-call(bf16[512,1920]{1,0:T(8,128)(2,1)S(1)} %get-tuple-element.17.summed, f32[8,128]{1,0:T(8,128)S(1)} %get-tuple-element.18.cols_in, ...), custom_call_target="tpu_custom_call" | custom-call | tf_op jit(solution)/shard_map/unpack/pallas_call | solution.py:786

commit v4 on v3

--- a/solution.py
+++ b/solution.py
@@ -25,7 +25,7 @@
 DEPTH = 8
 
 VALUE, CTX, HEAD, QUERY, KEY, SMALL, PAYLOAD = 0, 512, 640, 768, 1280, 1792, 1920
-CHUNKS = (((0, 384), (384, 768)), ((768, 1152), (1152, 1536)), ((1536, 1792), (1792, 1920)))
+CHUNKS = (((0, 384), (384, 768)), ((768, 1024), (1024, 1280)), ((1280, 1664), (1664, 1920)))
 
 Z2, POS, Z3, ROWS, COLS, UNIT, GZ2 = range(7)
 FIRST, SECOND, RING, SHARE_SECOND, SHARE_FIRST, CORE_OUT = (7 + 6 * n for n in range(6))
@@ -200,7 +200,7 @@
             s.context[2 * p + 1, :, lanes] = jnp.where(odd_row, context, 0.0)
         return carry
 
-    lax.fori_loop(0, PAIRS, one_pair, 0, unroll=True)
+    lax.fori_loop(0, PAIRS, one_pair, 0)
 
 def pool(wout, proj, s):
     context = jnp.concatenate([s.context[m] for m in range(MOLS)], axis=0)
@@ -242,7 +242,7 @@
         s.along[p] = along
         return carry
 
-    lax.fori_loop(0, PAIRS, one_pair, 0, unroll=True)
+    lax.fori_loop(0, PAIRS, one_pair, 0)
 
 
 def attend_backward(first, last, s):
@@ -271,7 +271,7 @@
         s.dks[p] = s.dk[...].astype(BF)
         return carry
 
-    lax.fori_loop(first, last, one_pair, 0, unroll=True)
+    lax.fori_loop(first, last, one_pair, 0)
 
 
 def bias_backward(s):
@@ -446,8 +446,8 @@
     logits = mm_t(z3_all, z2_all)
     expo = jnp.exp(logits)
     expo_t = jnp.exp(mm_t(z2_all, z3_all))
-    s.rows[plane] = jnp.broadcast_to(jnp.sum(expo_t, axis=0, keepdims=True), (8, LANES))
-    s.cols[depth] = jnp.broadcast_to(jnp.sum(expo, axis=0, keepdims=True), (8, LANES))
+    s.rows[plane] = jnp.sum(expo_t, axis=0, keepdims=True)
+    s.cols[depth] = jnp.sum(expo, axis=0, keepdims=True)
     start(rows_copy)
     start(cols_copy)
     lane = lax.broadcasted_iota(jnp.int32, (LANES, LANES), 1)
@@ -462,8 +462,8 @@
     for n in range(1, SIDE):
         row_sum = row_sum + s.rows[n]
         col_sum = col_sum + s.cols[n]
-    row_half = jnp.broadcast_to(0.5 / row_sum[0:1], (LANES, LANES)).T
-    slope = expo * (row_half + 0.5 / col_sum[0:1]) - jnp.where(hit, 1.0, 0.0)
+    row_half = jnp.broadcast_to(0.5 / row_sum, (LANES, LANES)).T
+    slope = expo * (row_half + 0.5 / col_sum) - jnp.where(hit, 1.0, 0.0)
     unit = mm(slope.astype(BF), z2_all)
     for n in range(SIDE):
         s.unit[n] = unit[n * 8 : (n + 1) * 8]
@@ -475,8 +475,8 @@
     s.gz2_in[depth] = s.gz2[depth]
     start(gz2_copy)
     one_lane = lax.broadcasted_iota(jnp.int32, (1, LANES), 1)
-    row_term = jnp.where((one_lane >> 3) == plane, 0.5 * jnp.log(row_sum[0:1]), 0.0)
-    col_term = jnp.where((one_lane >> 3) == depth, 0.5 * jnp.log(col_sum[0:1]), 0.0)
+    row_term = jnp.where((one_lane >> 3) == plane, 0.5 * jnp.log(row_sum), 0.0)
+    col_term = jnp.where((one_lane >> 3) == depth, 0.5 * jnp.log(col_sum), 0.0)
     loss_terms = row_term + col_term - score
 
     wait(s.unit_in.at[pl.ds(0, 15)], UNIT)
@@ -625,10 +625,10 @@
     first_step(0)
     attend_backward(2, PAIRS, s)
     project_backward(s.dqs, 0, QUERY, s)
+    core_copy(1).start()
     project_backward(s.dks, 1, KEY, s)
-    core_copy(1).start()
+    first_step(1)
     bias_backward(s)
-    first_step(1)
     gain_backward(wqkv, s)
     s.small[68:69, :] = loss_terms
     s.payload[:, SMALL:PAYLOAD] = s.small[...].astype(BF)
@@ -693,8 +693,8 @@
     "z2": ((LANES, LANES), F32),
     "pos": ((LANES, LANES), jnp.int32),
     "z3": ((LANES, LANES), F32),
-    "rows": ((SIDE, 8, LANES), F32),
-    "cols": ((SIDE, 8, LANES), F32),
+    "rows": ((SIDE, 1, LANES), F32),
+    "cols": ((SIDE, 1, LANES), F32),
     "unit": ((SIDE, 8, LANES), F32),
     "unit_in": ((SIDE, 8, LANES), F32),
     "gz2": ((SIDE, 8, LANES), F32),

time: 75.3 us -> 72.4 us (0.961)
  Pallas kernels: 74.3 us -> 71.5 us
    pallas_call x1, Pallas kernels: 71.3 us -> 68.5 us  [on_device(): pl.pallas_call(fused, out_shape=(pltpu.VMEM((WIDTH, PAYLOAD), BF), pltpu....]
where the time goes in v4:
time: 72.4 us; the launch traced here: 72.3 us
  Pallas kernels  71.5 us (99%)
  between operations  0.8 us (1%)
    pallas_call x1, Pallas kernels, on_device(): pl.pallas_call(fused, out_shape=(pltpu.VMEM((WIDTH, PAYLOAD), BF), pltpu....  68.5 us
    pallas_call x1, Pallas kernels, on_device(): pl.pallas_call(unpack, out_shape=tuple((jax.ShapeDtypeStruct(shape, F32)...  2.98 us

profile of v4, /device:TPU:1, one launch (start us, length us, event | category | flops | bytes accessed | tf_op | source)
XLA Modules:
  0.0 72.3 jit_solution(2314318354306550766)
XLA Ops:
  0.6 68.5 %pretrain_step.1 = (bf16[512,1920]{1,0:T(8,128)(2,1)S(1)}, f32[8,128]{1,0:T(8,128)S(1)}, bf16[512,128]{1,0:T(8,128)(2,1)S(1)}) custom-call(s32[8]{0:T(128)} %counts.1, s32[8]{0:T(128)} %positives.1, bf16[256,512]{1,0:T(8,128)(2,1)} %bitcast.7, f32[3,8,32]{2,1,0:T(8,128)} %bitcast.9, bf16[8,128]{1,0:T(8,128)(2,1)} %z2.1, bf16[512,1536]{1,0:T(8,128)(2,1)} %wqkv_in.1, ...), custom_call_target="tpu_custom_call" | custom-call | tf_op jit(solution)/shard_map/pretrain_step/pallas_call | solution.py:757
  69.1 3.0 %unpack.1 = (f32[1,1]{1,0:T(1,128)}, f32[8,128]{1,0:T(8,128)}, f32[512,1536]{1,0:T(8,128)}, f32[512,512]{1,0:T(8,128)}, f32[512,128]{1,0:T(8,128)}, /*index=5*/f32[64,128]{1,0:T(8,128)}, f32[1,512]{1,0:T(1,128)}) custom-call(bf16[512,1920]{1,0:T(8,128)(2,1)S(1)} %get-tuple-element.17.summed, f32[8,128]{1,0:T(8,128)S(1)} %get-tuple-element.18.cols_in, ...), custom_call_target="tpu_custom_call" | custom-call | tf_op jit(solution)/shard_map/unpack/pallas_call | solution.py:786

commit v5 on v4

--- a/solution.py
+++ b/solution.py
@@ -269,15 +269,17 @@
             for n, d in enumerate(ds_range):
                 s.dqs[p, :, pl.ds(d * LANES, LANES)] = (sums[n] * scale).astype(BF)
         s.dks[p] = s.dk[...].astype(BF)
+        s.bias_sum[...] = s.bias_sum[...] + mm(s.basis[p], s.attn[p].astype(BF))
         return carry
 
+    if first == 0:
+        s.bias_sum[...] = jnp.zeros((2 * KERNELS, LANES), F32)
+
     lax.fori_loop(first, last, one_pair, 0)
 
 
 def bias_backward(s):
-    bias_sum = jnp.zeros((2 * KERNELS, LANES), F32)
-    for p in range(PAIRS):
-        bias_sum = bias_sum + mm(s.basis[p], s.attn[p].astype(BF))
+    bias_sum = s.bias_sum[...]
     odd = lane_is_odd((KERNELS, LANES))
     folded = jnp.where(odd, bias_sum[KERNELS:], bias_sum[:KERNELS]).T
     s.small[...] = jnp.zeros((WIDTH, LANES), F32)
@@ -314,9 +316,11 @@
     proj_in,
     bias_t,
     gain,
-    summed,
+    qkv,
+    out,
+    head,
+    small,
     grad_z2,
-    proj,
     *scratch,
 ):
     s = Scratch(scratch)
@@ -324,12 +328,12 @@
     loads = [
         pltpu.make_async_copy(src, dst, s.load.at[n])
         for n, (src, dst) in enumerate(
-            ((feats_in, s.feats), (wqkv_in, s.wqkv), (wout_in, s.wout), (proj_in, proj))
+            ((feats_in, s.feats), (wqkv_in, s.wqkv), (wout_in, s.wout), (proj_in, s.proj))
         )
     ]
     for load in loads:
         load.start()
-    feats, wqkv, wout = s.feats, s.wqkv, s.wout
+    feats, wqkv, wout, proj, summed = s.feats, s.wqkv, s.wout, s.proj, s.summed
 
     dp, y_high = lax.axis_index("dp"), lax.axis_index("group")
     bits = [(dp // 2**n) % 2 for n in range(7)]
@@ -649,8 +653,12 @@
     share_first_step(2)
     share_core_step(1)
     arrive_step(0)
+    qkv[:, 2 * WIDTH : 3 * WIDTH] = summed[:, VALUE:CTX].astype(F32)
+    out[...] = mm_t(summed[:, CTX:HEAD], proj[...])
+    head[...] = summed[:, HEAD:QUERY].astype(F32)
     share_core_step(2)
     arrive_step(1)
+    qkv[:, 0:WIDTH] = summed[:, QUERY:KEY].astype(F32)
 
     wait(s.gz2_in.at[pl.ds(0, 15)], GZ2)
     total = s.gz2_in[0]
@@ -658,6 +666,8 @@
         total = total + s.gz2_in[n]
     grad_z2[...] = total
     arrive_step(2)
+    qkv[:, WIDTH : 2 * WIDTH] = summed[:, KEY:SMALL].astype(F32)
+    small[...] = summed[0:80, SMALL:PAYLOAD].astype(F32)
     for c in range(3):
         core_copy(c).wait_send()
         for h in range(2):
@@ -679,6 +689,7 @@
     "basis": ((PAIRS, 2 * KERNELS, ATOMS * ATOMS), BF),
     "attn": ((PAIRS, ATOMS * ATOMS, LANES), F32),
     "column": ((PAIRS, ATOMS, LANES), F32),
+    "bias_sum": ((2 * KERNELS, LANES), F32),
     "context": ((MOLS, 1, WIDE), F32),
     "ctx_sum": ((MOLS, WIDTH), F32),
     "pooled": ((MOLS, WIDTH), F32),
@@ -709,6 +720,8 @@
     "feats": ((256, WIDTH), BF),
     "wqkv": ((WIDTH, 3 * WIDTH), BF),
     "wout": ((WIDTH, WIDTH), BF),
+    "proj": ((WIDTH, LANES), BF),
+    "summed": ((WIDTH, PAYLOAD), BF),
 }
 
 
@@ -719,7 +732,7 @@
 
 
 def unpack(
-    summed, cols_in, proj, loss, cols_out, g_qkv, g_out, g_proj, g_bias, g_gain, qkv, out, head, sems
+    qkv, out, head, small, cols_in, loss, cols_out, g_qkv, g_out, g_proj, g_bias, g_gain, sems
 ):
     copies = []
 
@@ -728,22 +741,15 @@
         copies[-1].start()
 
     for n in range(4):
-        at = pl.ds(n * 128, 128)
-        for part, start in enumerate((QUERY, KEY, VALUE)):
-            qkv[at, part * WIDTH : (part + 1) * WIDTH] = summed[at, start : start + WIDTH].astype(F32)
-        store(qkv.at[at, :], g_qkv.at[at, :])
+        store(qkv.at[pl.ds(n * 128, 128), :], g_qkv.at[pl.ds(n * 128, 128), :])
     for n in range(2):
-        at = pl.ds(n * 256, 256)
-        out[at, :] = mm_t(summed[at, CTX:HEAD], proj[...])
-        store(out.at[at, :], g_out.at[at, :])
-    head[...] = summed[:, HEAD:QUERY].astype(F32)
+        store(out.at[pl.ds(n * 256, 256), :], g_out.at[pl.ds(n * 256, 256), :])
     store(head, g_proj)
     cols_out[...] = cols_in[...]
-    g_bias[...] = summed[0:64, SMALL:PAYLOAD].astype(F32)
-    small = summed[64:80, SMALL:PAYLOAD].astype(F32)
+    g_bias[...] = small[0:64, :]
     for n in range(4):
-        g_gain[:, n * LANES : (n + 1) * LANES] = small[n : n + 1]
-    loss[...] = jnp.sum(small[4:5], axis=1, keepdims=True) / BATCH
+        g_gain[:, n * LANES : (n + 1) * LANES] = small[64 + n : 65 + n, :]
+    loss[...] = jnp.sum(small[68:69, :], axis=1, keepdims=True) / BATCH
     for copy in copies:
         copy.wait()
 
@@ -754,15 +760,17 @@
     vmem = pl.BlockSpec(memory_space=pltpu.VMEM)
     smem = pl.BlockSpec(memory_space=pltpu.SMEM)
     hbm = pl.BlockSpec(memory_space=pl.ANY)
-    summed, grad_z2, proj_near = pl.pallas_call(
+    left = pl.pallas_call(
         fused,
         out_shape=(
-            pltpu.VMEM((WIDTH, PAYLOAD), BF),
+            pltpu.VMEM((WIDTH, 3 * WIDTH), F32),
+            pltpu.VMEM((WIDTH, WIDTH), F32),
+            pltpu.VMEM((WIDTH, LANES), F32),
+            pltpu.VMEM((80, LANES), F32),
             pltpu.VMEM((8, LANES), F32),
-            pltpu.VMEM((WIDTH, LANES), BF),
         ),
         in_specs=[smem, smem, hbm, vmem, vmem, hbm, hbm, hbm, vmem, vmem],
-        out_specs=(vmem, vmem, vmem),
+        out_specs=(vmem,) * 5,
         scratch_shapes=[pltpu.VMEM(*shape) for shape in SHAPES.values()]
         + [pltpu.SemaphoreType.DMA((KINDS,))] * 2
         + [pltpu.SemaphoreType.DMA((4,))],
@@ -786,17 +794,12 @@
     loss, grad_z2, g_qkv, g_out, g_proj, g_bias, g_gain = pl.pallas_call(
         unpack,
         out_shape=tuple(jax.ShapeDtypeStruct(shape, F32) for shape in shapes),
-        in_specs=[vmem, vmem, vmem],
+        in_specs=[vmem] * 5,
         out_specs=(vmem, vmem, hbm, hbm, hbm, vmem, vmem),
-        scratch_shapes=[
-            pltpu.VMEM((WIDTH, 3 * WIDTH), F32),
-            pltpu.VMEM((WIDTH, WIDTH), F32),
-            pltpu.VMEM((WIDTH, LANES), F32),
-            pltpu.SemaphoreType.DMA((7,)),
-        ],
+        scratch_shapes=[pltpu.SemaphoreType.DMA((7,))],
         compiler_params=pltpu.CompilerParams(vmem_limit_bytes=32 * 1024 * 1024),
         name="unpack",
-    )(summed, grad_z2, proj_near)
+    )(*left)
     return (loss.reshape(()), grad_z2, g_qkv, g_out, g_proj, g_bias.T, g_gain.reshape(WIDTH))
 
 

time: 72.4 us -> 73.5 us (1.015)
  Pallas kernels: 71.5 us -> 72.5 us
    pallas_call x1, Pallas kernels: 68.5 us -> 69.7 us  [on_device(): pl.pallas_call(fused, out_shape=(pltpu.VMEM((WIDTH, 3 * WIDTH), F32), plt...]
where the time goes in v5:
time: 73.5 us; the launch traced here: 73.3 us
  Pallas kernels  72.5 us (99%)
  between operations  0.8 us (1%)
    pallas_call x1, Pallas kernels, on_device(): pl.pallas_call(fused, out_shape=(pltpu.VMEM((WIDTH, 3 * WIDTH), F32), plt...  69.7 us
    pallas_call x1, Pallas kernels, on_device(): pl.pallas_call(unpack, out_shape=tuple((jax.ShapeDtypeStruct(shape, F32)...  2.77 us

profile of v5, /device:TPU:1, one launch (start us, length us, event | category | flops | bytes accessed | tf_op | source)
XLA Modules:
  0.0 73.3 jit_solution(8870664320746994053)
XLA Ops:
  0.6 69.7 %pretrain_step.1 = (f32[512,1536]{1,0:T(8,128)S(1)}, f32[512,512]{1,0:T(8,128)S(1)}, f32[512,128]{1,0:T(8,128)S(1)}, f32[80,128]{1,0:T(8,128)S(1)}, f32[8,128]{1,0:T(8,128)S(1)}) custom-call(s32[8]{0:T(128)} %counts.1, s32[8]{0:T(128)} %positives.1, bf16[256,512]{1,0:T(8,128)(2,1)} %bitcast.7, f32[3,8,32]{2,1,0:T(8,128)} %bitcast.9, bf16[8,128]{1,0:T(8,128)(2,1)} %z2.1, ...), custom_call_target="tpu_custom_call" | custom-call | tf_op jit(solution)/shard_map/pretrain_step/pallas_call | solution.py:763
  70.4 2.8 %unpack.1 = (f32[1,1]{1,0:T(1,128)}, f32[8,128]{1,0:T(8,128)}, f32[512,1536]{1,0:T(8,128)}, f32[512,512]{1,0:T(8,128)}, f32[512,128]{1,0:T(8,128)}, /*index=5*/f32[64,128]{1,0:T(8,128)}, f32[1,512]{1,0:T(1,128)}) custom-call(f32[512,1536]{1,0:T(8,128)S(1)} %get-tuple-element.19.qkv, f32[512,512]{1,0:T(8,128)S(1)} %get-tuple-element.20.out, ...), custom_call_target="tpu_custom_call" | custom-call | tf_op jit(solution)/shard_map/unpack/pallas_call | solution.py:794
